TPU v7x, 256 devices: a whole 4x4x8 slice. The times are simulated.
256 devices in a mesh: cls: 4 (over x_lo, core), row: 64 (over x_hi, z, y).
Axes of the slice: x: 4 (x_hi: 2, x_lo: 2; x = x_hi * 2 + x_lo), y: 4, z: 8, core: 2. Of those that a mesh axis runs over, the one named last changes fastest.
Arguments:
- scores: float32 [16384, 64], P('row', 'cls'), may hold values from -30 to 280
- labels: int32 [16384], P('row'), may hold values from 0 to 63
- nodes: int32 [16384, 64], P('row', 'cls'), may hold values from 0 to 3
- bins: int32 [16384, 256], P('row'), may hold values from 0 to 127
- pick_feature: int32 [64, 4], P('cls'), may hold values from 0 to 255
- pick_bin: int32 [64, 4], P('cls'), may hold values from 0 to 126
Outputs:
- best_gain: float32 [64, 4], P('cls')
- new_scores: float32 [16384, 64], P('row', 'cls')
All inputs are finite; a program needn't handle non-finite values.
Results may differ from a plain program's by a relative error of at most 0.0014.
Values sent between devices are 32-bit elements; how exact they have to be, the bound alone decides.
No kernel may reach another device: no remote copies, remote signals or barrier semaphores. Data moves between devices by JAX's collectives and lax.ppermute only.
A program may use at most 128 MiB of HBM per device.

v0:
```python
import math

import jax
import jax.numpy as jnp
from jax import lax
from jax.sharding import PartitionSpec as P

BINS = 128


reg_lambda = 1.0
learn_rate = 0.5


def per_device(scores, labels, nodes, bins, pick_feature, pick_bin):
    row_count, class_count = scores.shape
    node_count = pick_feature.shape[1]
    feature_count = bins.shape[1]
    feature_share = feature_count // lax.axis_size("row")
    local_top = jnp.max(scores, axis=1)
    highest = lax.pmax(local_top, "cls")
    exponent = jnp.exp(scores - highest[:, None])
    denominator = lax.psum(jnp.sum(exponent, axis=1), "cls")
    prob = exponent / denominator[:, None]
    class_start = lax.axis_index("cls") * class_count
    class_range = class_start + jnp.arange(class_count, dtype=jnp.int32)
    target = (labels[:, None] == class_range[None, :]).astype(jnp.float32)
    gradient = (prob - target).astype(jnp.bfloat16)
    hessian = (2.0 * prob * (1.0 - prob)).astype(jnp.bfloat16)
    node_mask = nodes[:, :, None] == jnp.arange(node_count, dtype=jnp.int32)[None, None, :]
    zero_half = jnp.zeros((), jnp.bfloat16)
    paired = jnp.stack(
        [
            jnp.where(node_mask, gradient[:, :, None], zero_half),
            jnp.where(node_mask, hessian[:, :, None], zero_half),
        ],
        axis=-1,
    )
    paired = paired.reshape(row_count, class_count * node_count * 2)
    column_count = paired.shape[1]
    bin_range = jnp.arange(BINS, dtype=jnp.int32)
    feature_block = feature_share * BINS * lax.axis_size("row") // BINS
    group = math.gcd(feature_block, 16)

    def one_group(number):
        picked = lax.dynamic_slice_in_dim(bins, number * group, group, 1)
        onehot = (picked[:, :, None] == bin_range[None, None, :]).astype(jnp.bfloat16)
        onehot = onehot.reshape(row_count, group * BINS)
        return lax.dot_general(
            onehot, paired, (((0,), (0,)), ((), ())), preferred_element_type=jnp.float32
        )

    blocks = lax.map(one_group, jnp.arange(feature_block // group, dtype=jnp.int32))
    owned = lax.psum_scatter(
        blocks.reshape(feature_share * BINS * lax.axis_size("row"), column_count),
        "row",
        scatter_dimension=0,
        tiled=True,
    )
    owned = owned.reshape(feature_share, BINS, class_count, node_count, 2)
    running = jnp.cumsum(owned, axis=1)
    grad_total = running[:, -1:, :, :, 0]
    hess_total = running[:, -1:, :, :, 1]
    grad_left = running[:, :-1, :, :, 0]
    hess_left = running[:, :-1, :, :, 1]
    gain = 0.5 * (
        grad_left * grad_left / (hess_left + reg_lambda)
        + (grad_total - grad_left) ** 2 / (hess_total - hess_left + reg_lambda)
        - grad_total * grad_total / (hess_total + reg_lambda)
    )
    local_best = jnp.max(gain, axis=(0, 1))
    feature_ids = lax.axis_index("row") * feature_share + jnp.arange(feature_share, dtype=jnp.int32)
    chosen = pick_feature[None, :, :] == feature_ids[:, None, None]
    bin_hot = (bin_range[:, None, None] == pick_bin[None, :, :]).astype(jnp.float32)
    at_pick = jnp.sum(running * bin_hot[None, :, :, :, None], axis=1)
    stacked = jnp.concatenate([at_pick, running[:, -1]], axis=-1)
    local_stats = jnp.sum(jnp.where(chosen[:, :, :, None], stacked, 0.0), axis=0)
    best_gain = lax.pmax(local_best, "row")
    split_sums = lax.psum(local_stats, "row")
    left_weight = -split_sums[:, :, 0] / (split_sums[:, :, 1] + reg_lambda)
    right_weight = -(split_sums[:, :, 2] - split_sums[:, :, 0]) / (
        split_sums[:, :, 3] - split_sums[:, :, 1] + reg_lambda
    )
    row_feature = jnp.sum(jnp.where(node_mask, pick_feature[None, :, :], 0), axis=2)
    row_bin = jnp.sum(jnp.where(node_mask, pick_bin[None, :, :], 0), axis=2)
    row_left = jnp.sum(jnp.where(node_mask, left_weight[None, :, :], 0.0), axis=2)
    row_right = jnp.sum(jnp.where(node_mask, right_weight[None, :, :], 0.0), axis=2)
    value_at = jnp.take_along_axis(bins, row_feature, axis=1)
    leaf = jnp.where(value_at <= row_bin, row_left, row_right)
    return (best_gain, scores + learn_rate * leaf)


def solution(mesh):
    in_specs = (
        P("row", "cls"),
        P("row"),
        P("row", "cls"),
        P("row", None),
        P("cls", None),
        P("cls", None),
    )
    out_specs = (P("cls", None), P("row", "cls"))
    return jax.shard_map(
        per_device, mesh=mesh, in_specs=in_specs, out_specs=out_specs, check_vma=False
    )
```

profile of v0, /device:TPU:8, one launch (start us, length us, event | category | flops | bytes accessed | tf_op | source)
XLA Modules:
  0.0 1115.9 jit_solution(5143679266849984362)
XLA Ops:
  7.2 0.7 reduce_max.18
  8.0 6.9 pmax.14
  14.9 0.7 fusion.23
  15.6 5.9 psum.14
  21.5 0.8 subtract_convert_fusion
  22.3 0.8 compare_select_fusion.1
  23.4 77.9 %while.11 = (s32[]{:T(128)}, f32[16,2048,128]{2,1,0:T(8,128)}, s32[16]{0:T(128)S(1)}, s32[256,256]{1,0:T(8,128)}, bf16[256,128]{1,0:T(8,128)(2,1)S(1)}, /*index=5*/s32[]{:T(128)}, s32[1]{0:T(128)}, s32[]{:T(128)}, s32[]{:T(128)}) while((s32[]{:T(128)}, f32[16,2048,128]{2,1,0:T(8,128)}, s32[16]{0:T(128)S(1)}, s32[256,256]{1,0:T(8,128)}, ...), condition=%wide.region_5.6_spmd.clone, body=%wide.region_4.5_spmd.clone.sunk | while | flops 134742016 | bytes 5374119 | solution.py:53
  24.7 1.0 constant_dynamic-slice_fusion.2
  25.7 0.6 eq.170
  26.3 2.0 fusion.31
  29.6 1.0 constant_dynamic-slice_fusion.2
  30.6 0.6 eq.170
  31.2 2.0 fusion.31
  34.5 1.0 constant_dynamic-slice_fusion.2
  35.5 0.6 eq.170
  36.1 2.0 fusion.31
  39.3 1.0 constant_dynamic-slice_fusion.2
  40.3 0.6 eq.170
  41.0 2.0 fusion.31
  44.2 1.0 constant_dynamic-slice_fusion.2
  45.2 0.6 eq.170
  45.8 2.0 fusion.31
  49.0 1.0 constant_dynamic-slice_fusion.2
  50.0 0.6 eq.170
  50.7 2.0 fusion.31
  53.9 1.0 constant_dynamic-slice_fusion.2
  54.9 0.6 eq.170
  55.5 2.0 fusion.31
  58.8 1.0 constant_dynamic-slice_fusion.2
  59.8 0.6 eq.170
  60.4 2.0 fusion.31
  63.6 1.0 constant_dynamic-slice_fusion.2
  64.7 0.6 eq.170
  65.3 2.1 fusion.31
  68.6 1.0 constant_dynamic-slice_fusion.2
  69.6 0.6 eq.170
  70.2 2.0 fusion.31
  73.4 1.0 constant_dynamic-slice_fusion.2
  74.4 0.6 eq.170
  75.0 2.0 fusion.31
  78.3 1.0 constant_dynamic-slice_fusion.2
  79.9 2.0 fusion.31
  83.1 1.0 constant_dynamic-slice_fusion.2
  84.7 2.1 fusion.31
  88.0 1.0 constant_dynamic-slice_fusion.2
  89.6 2.0 fusion.31
  92.9 1.0 constant_dynamic-slice_fusion.2
  94.5 2.0 fusion.31
  97.7 1.0 constant_dynamic-slice_fusion.2
  99.3 2.0 fusion.31
  101.3 17.4 %copy.87 = f32[32768,128]{0,1:T(8,128)} copy(f32[32768,128]{1,0:T(8,128)} %bitcast.67) | data formatting | bytes 33554432 | tf_op jit(solution)/shard_map/reshape | solution.py:55
  118.8 0.7 copy-done.2
  119.8 32.8 %gather_fusion = s32[4096]{0:T(1024)S(1)} fusion(s32[256,256]{1,0:T(8,128)S(1)} %copy-done, s32[4096]{0:T(1024)S(1)} %reshape.136), kind=kCustom, calls=%fused_computation | custom fusion | bytes 65536 | tf_op jit(solution)/shard_map/jit(take_along_axis)/gather | solution.py:88
  152.9 363.1 %reduce-scatter.2.cloned.1.call-done = f32[512,128]{0,1:T(8,128)} async-done(((f32[32768,128]{0,1:T(8,128)}), f32[512,128]{0,1:T(8,128)}) %reduce-scatter.2.cloned.1.call-update) | async-done | bytes 262160 | tf_op jit(solution)/shard_map/reduce_scatter | solution.py:54
  516.0 1.0 reshape.135
  517.1 8.9 copy.88
  526.0 6.5 fusion.25
  532.7 12.2 %fusion.24 = (f32[4,127,16,4,1]{4,2,3,1,0:T(8,128)}, f32[4,127,16,4,1]{4,2,3,1,0:T(8,128)}) fusion(f32[4,128,16,4,2]{4,2,3,1,0:T(8,128)S(1)} %fusion.25), kind=kLoop, calls=%fused_computation.60 | loop fusion | bytes 520192 | tf_op jit(solution)/shard_map/slice | solution.py:64
  544.9 2.4 multiply_reduce_fusion
  547.8 350.6 %psum.15 = f32[16,4,4]{2,0,1:T(8,128)S(1)} all-reduce(f32[16,4,4]{2,0,1:T(8,128)S(1)} %copy.96), channel_id=1, replica_groups=mesh['cls'=4,'row'=64] {'row'}, use_global_device_ids=true, to_apply=%region_14.15 | all-reduce | flops 256 | bytes 2048 | tf_op jit(solution)/shard_map/psum | solution.py:79
  898.6 12.3 %copy.89 = f32[4,127,16,4,1]{1,2,4,3,0:T(8,128)S(1)} copy(f32[4,127,16,4,1]{4,2,3,1,0:T(8,128)} %get-tuple-element.105) | data formatting | bytes 260096 | tf_op jit(solution)/shard_map/slice | solution.py:64
  910.8 12.3 %copy.90 = f32[4,127,16,4,1]{1,2,4,3,0:T(8,128)S(1)} copy(f32[4,127,16,4,1]{4,2,3,1,0:T(8,128)} %get-tuple-element.106) | data formatting | bytes 260096 | tf_op jit(solution)/shard_map/slice | solution.py:65
  923.3 185.0 %pmax.15 = f32[16,4]{0,1:T(4,128)} all-reduce(f32[16,4]{0,1:T(4,128)S(1)} %fusion.12), channel_id=1, replica_groups=mesh['cls'=4,'row'=64] {'row'}, use_global_device_ids=true, to_apply=%region_9.10 | all-reduce | flops 64 | bytes 512 | tf_op jit(solution)/shard_map/pmax | solution.py:78
  1108.4 0.6 multiply_add_fusion
  (73 shorter events, 14.6 us)
Async XLA Ops:
  7.2 508.9 %reduce-scatter.2.cloned.1.call-start = ((), (), s32[]{:S(2)}) async-start(), calls=%async_computation.1 | async-start | bytes 17039360 | tf_op jit(solution)/shard_map/reduce_scatter | solution.py:54
  118.8 0.7 copy-start.2
  118.8 0.7 copy-start.3
  118.8 0.7 copy-start.4
  118.8 1.0 copy-start
  898.5 209.9 %copy-start.1 = (f32[256,16]{0,1:T(8,128)S(1)}, f32[256,16]{0,1:T(8,128)}, u32[]{:S(2)}) copy-start(f32[256,16]{0,1:T(8,128)} %param.8) | copy-start | bytes 49156
Sparse Core Ops, SparseCore 0:
  118.9 397.0 reduce-scatter.1
where the time goes:
time: 1120 us
  blocking collectives  548 us (49%)
  waiting for transfers between devices  363 us (32%)
  local copies, waits for them, and re-layouts  134 us (12%)
  matrix products  32.1 us (3%)
  between operations  14.2 us (1%)
  other arithmetic  13.5 us (1%)
    reduce_scatter x1, waiting for transfers between devices, per_device(): lax.psum_scatter(blocks.reshape(feature_share * BINS * lax.axis_size('row...  363 us
    psum x1, blocking collectives, per_device(): split_sums = lax.psum(local_stats, 'row')  351 us
    pmax x1, blocking collectives, per_device(): best_gain = lax.pmax(local_best, 'row')  185 us
    gather x5, local copies, waits for them, and re-layouts, per_device(): value_at = jnp.take_along_axis(bins, row_feature, axis=1)  33.1 us
    dot_general x16, matrix products, one_group(): lax.dot_general(onehot, paired, (((0,), (0,)), ((), ())), preferred_eleme...  32.1 us
    slice x2, local copies, waits for them, and re-layouts, per_device(): grad_left = running[:, :-1, :, :, 0]  24.5 us
  transfers between devices with their start and end apart: 1, of which 1 were waited for; matrix products, arithmetic and copies ran while one was open for 3% of the time, Pallas kernels for 0%

commit v1 on v0

v1 whole, which is shorter than its diff:
```python
import jax
import jax.numpy as jnp
from jax import lax
from jax.experimental import pallas as pl
from jax.experimental.pallas import tpu as pltpu
from jax.sharding import Mesh, PartitionSpec as P

BINS = 128
NODES = 4
SHARD = 16
HALF = 128
GROUPS = 32
FEATS = 8
PART = 8

reg_lambda = 1.0
learn_rate = 0.5

CLS = ("xl", "core")
ROW = ("xh", "z", "y")
VMEM = pl.BlockSpec(memory_space=pltpu.VMEM)
SMEM = pl.BlockSpec(memory_space=pltpu.SMEM)


def params(mib):
    return pltpu.CompilerParams(vmem_limit_bytes=mib * 1024 * 1024)


def prepare_kernel(place, every, labels, bins, send):
    xl, core = place[0], place[1]

    def half(x):
        return jnp.where(core == 0, x[..., :HALF], x[..., HALF:])

    scores = [half(every[i, :SHARD, :]) for i in range(4)]
    nodes = [half(every[i, SHARD:, :]) for i in range(4)]
    label = half(labels[...])
    top = jnp.max(jnp.maximum(jnp.maximum(scores[0], scores[1]), jnp.maximum(scores[2], scores[3])), axis=0, keepdims=True)
    exponent = [jnp.exp(s - top) for s in scores]
    denominator = jnp.sum((exponent[0] + exponent[1]) + (exponent[2] + exponent[3]), axis=0, keepdims=True)
    prob = [jnp.where(xl == 0, exponent[i], exponent[2 + i]) / denominator for i in range(2)]
    node = [jnp.where(xl == 0, nodes[i], nodes[2 + i]) for i in range(2)]
    columns = bins[pl.ds(pl.multiple_of(core * HALF, HALF), HALF), :].astype(jnp.float32).T
    label_rows = jnp.broadcast_to(label, (8, HALF))
    for q in range(2):
        part = slice(q * PART, (q + 1) * PART)
        for group in range(GROUPS):
            where = q * GROUPS + group
            send[where, 0:8] = prob[0][part]
            send[where, 8:16] = prob[1][part]
            send[where, 16:24] = node[0][part]
            send[where, 24:32] = node[1][part]
            send[where, 32:40] = columns[group * FEATS : (group + 1) * FEATS]
            send[where, 40:48] = label_rows


def route_kernel(picks, nodes, bins, route):
    pick = picks[...]
    column = jnp.concatenate([pick[:, n : n + 1] for n in range(NODES)], axis=0)
    features = bins.shape[1]
    hot = (lax.broadcasted_iota(jnp.int32, (NODES * SHARD, features), 1) == (column // BINS)).astype(jnp.bfloat16)
    value = lax.dot_general(
        hot, bins[...].astype(jnp.bfloat16), (((1,), (1,)), ((), ())), preferred_element_type=jnp.float32
    )
    right = (value > (column % BINS).astype(jnp.float32)).astype(jnp.int32)
    node = nodes[...]
    out = 2 * node
    for n in range(NODES):
        out = out + jnp.where(node == n, right[n * SHARD : (n + 1) * SHARD], 0)
    route[...] = out


CHUNK = 8


def left_kernel(place, taken, left, paired, mask):
    xl, quarter = place[0], place[2]
    lane_class = lax.broadcasted_iota(jnp.int32, (PART, HALF), 0) + quarter * PART
    ids = [(lane_class + (2 * xl + shard) * SHARD).astype(jnp.float32) for shard in range(2)]
    bin_range = lax.broadcasted_iota(jnp.int32, (BINS, HALF), 0).astype(jnp.bfloat16)
    one, zero = jnp.ones((), jnp.bfloat16), jnp.zeros((), jnp.bfloat16)

    @pl.loop(0, taken.shape[0] // CHUNK)
    def _(chunk):
        for step in range(CHUNK):
            source = chunk * CHUNK + step
            lanes = slice(step * HALF, (step + 1) * HALF)
            label = taken[source, 40:48]
            for shard in range(2):
                prob = taken[source, shard * 8 : shard * 8 + 8]
                node = taken[source, 16 + shard * 8 : 24 + shard * 8]
                target = (label == ids[shard]).astype(jnp.float32)
                values = ((prob - target), 2.0 * prob * (1.0 - prob))
                for pair in range(2):
                    tile = jnp.concatenate([jnp.where(node == float(n), values[pair], 0.0) for n in range(NODES)], axis=0)
                    first = shard * 64 + pair * 32
                    paired[first : first + 32, lanes] = tile.astype(jnp.bfloat16)
            for f in range(FEATS):
                row = jnp.broadcast_to(taken[source, 32 + f : 33 + f], (BINS, HALF)).astype(jnp.bfloat16)
                mask[f * BINS : (f + 1) * BINS, lanes] = jnp.where(bin_range >= row, one, zero)
        product = lax.dot_general(
            paired[...], mask[...], (((1,), (1,)), ((), ())), preferred_element_type=jnp.float32
        )

        @pl.when(chunk == 0)
        def _():
            left[...] = product

        @pl.when(chunk > 0)
        def _():
            left[...] += product


def gain_kernel(place, own, other, target, spread):
    group = place[3]
    rows = NODES * PART
    grad = own[:rows] + other[:rows]
    hess = own[rows:] + other[rows:]
    pick = target[...] - group * (FEATS * BINS)
    lane = lax.broadcasted_iota(jnp.int32, (rows, BINS), 1)
    best = None
    sums = [jnp.zeros((rows, BINS), jnp.float32) for _ in range(2)]
    totals = [jnp.zeros((rows, 1), jnp.float32) for _ in range(2)]
    for f in range(FEATS):
        g = grad[:, f * BINS : (f + 1) * BINS]
        h = hess[:, f * BINS : (f + 1) * BINS]
        gt = g[:, BINS - 1 :]
        ht = h[:, BINS - 1 :]
        gain = 0.5 * (g * g / (h + reg_lambda) + (gt - g) ** 2 / (ht - h + reg_lambda) - gt * gt / (ht + reg_lambda))
        gain = jnp.where(lane == BINS - 1, -jnp.inf, gain)
        best = gain if best is None else jnp.maximum(best, gain)
        here = lane + f * BINS == pick
        inside = (pick >= f * BINS) & (pick < (f + 1) * BINS)
        for i, (x, t) in enumerate(((g, gt), (h, ht))):
            sums[i] = jnp.where(here, x, sums[i])
            totals[i] = jnp.where(inside, t, totals[i])
    columns = [
        jnp.max(best, axis=1, keepdims=True),
        jnp.sum(sums[0], axis=1, keepdims=True),
        jnp.sum(sums[1], axis=1, keepdims=True),
        totals[0],
        totals[1],
    ]
    lane8 = lax.broadcasted_iota(jnp.int32, (PART, BINS), 1)
    tile = jnp.zeros((PART, BINS), jnp.float32)
    for j, column in enumerate(columns):
        for n in range(NODES):
            tile = jnp.where(lane8 == j * NODES + n, column[n * PART : (n + 1) * PART], tile)
    spread[...] = jnp.broadcast_to(tile[None], spread.shape)


def finish_kernel(gathered, scores, route, best, new_scores):
    top, total = [], []
    for q in range(2):
        block = gathered[q * GROUPS : (q + 1) * GROUPS]
        top.append(jnp.max(block, axis=0))
        total.append(jnp.sum(block, axis=0))
    top = jnp.concatenate(top, axis=0)
    total = jnp.concatenate(total, axis=0)
    best[...] = top.T[:NODES, :SHARD]
    grad_left, hess_left, grad_total, hess_total = (total[:, 4 * j : 4 * j + 4] for j in range(1, 5))
    left = -grad_left / (hess_left + reg_lambda)
    right = -(grad_total - grad_left) / (hess_total - hess_left + reg_lambda)
    way = route[...]
    leaf = jnp.zeros(way.shape, jnp.float32)
    for n in range(NODES):
        leaf = jnp.where(way == 2 * n, left[:, n : n + 1], leaf)
        leaf = jnp.where(way == 2 * n + 1, right[:, n : n + 1], leaf)
    new_scores[...] = scores[...] + learn_rate * leaf


def per_device(scores, labels, nodes, bins, pick_feature, pick_bin):
    xl, core, xh = (lax.axis_index(a) for a in ("xl", "core", "xh"))
    group = lax.axis_index("z") * lax.axis_size("y") + lax.axis_index("y")
    place = jnp.stack([xl, core, xh, group]).astype(jnp.int32)
    chips = 2 * GROUPS
    scores_t, nodes_t = scores.T, nodes.T
    picks = pick_feature * BINS + pick_bin
    f32 = jnp.float32

    every = lax.all_gather(jnp.concatenate([scores_t, nodes_t.astype(f32)], axis=0), CLS)
    send = pl.pallas_call(
        prepare_kernel,
        out_shape=jax.ShapeDtypeStruct((chips, 48, HALF), f32),
        in_specs=[SMEM, VMEM, VMEM, VMEM],
        out_specs=VMEM,
        compiler_params=params(16),
        name="prepare",
    )(place, every, labels.astype(f32)[None], bins)
    route = pl.pallas_call(
        route_kernel,
        out_shape=jax.ShapeDtypeStruct((SHARD, 2 * HALF), jnp.int32),
        in_specs=[VMEM] * 3,
        out_specs=VMEM,
        compiler_params=params(16),
        name="route",
    )(picks, nodes_t, bins)
    taken = lax.all_to_all(send, ROW, 0, 0)
    left = pl.pallas_call(
        left_kernel,
        out_shape=jax.ShapeDtypeStruct((128, FEATS * BINS), f32),
        in_specs=[SMEM, VMEM],
        out_specs=VMEM,
        scratch_shapes=[
            pltpu.VMEM((128, CHUNK * HALF), jnp.bfloat16),
            pltpu.VMEM((FEATS * BINS, CHUNK * HALF), jnp.bfloat16),
        ],
        compiler_params=params(32),
        name="left",
    )(place, taken)
    halves = left.reshape(2, 64, FEATS * BINS)
    own = lax.dynamic_index_in_dim(halves, core, 0, keepdims=False)
    away = lax.dynamic_index_in_dim(halves, 1 - core, 0, keepdims=False)
    other = lax.ppermute(away, "core", [(0, 1), (1, 0)])
    target = lax.dynamic_slice_in_dim(picks, xh * PART, PART, 0).T.reshape(NODES * PART, 1)
    spread = pl.pallas_call(
        gain_kernel,
        out_shape=jax.ShapeDtypeStruct((chips, PART, BINS), f32),
        in_specs=[SMEM, VMEM, VMEM, VMEM],
        out_specs=VMEM,
        compiler_params=params(16),
        name="gain",
    )(place, own, other, target)
    gathered = lax.all_to_all(spread, ROW, 0, 0)
    best, new_scores = pl.pallas_call(
        finish_kernel,
        out_shape=(jax.ShapeDtypeStruct((NODES, SHARD), f32), jax.ShapeDtypeStruct((SHARD, 2 * HALF), f32)),
        in_specs=[VMEM] * 3,
        out_specs=(VMEM, VMEM),
        compiler_params=params(16),
        name="finish",
    )(gathered, scores_t, route)
    return best.T, new_scores.T


def solution(mesh):
    fine = Mesh(mesh.devices.reshape(2, 2, 2, 8, 4), CLS + ROW)
    in_specs = (P(ROW, CLS), P(ROW), P(ROW, CLS), P(ROW, None), P(CLS, None), P(CLS, None))
    out_specs = (P(CLS, None), P(ROW, CLS))
    return jax.shard_map(per_device, mesh=fine, in_specs=in_specs, out_specs=out_specs, check_vma=False)
```

time: 1120 us -> 101 us (0.09)
  blocking collectives: 548 us -> 5.41 us
  waiting for transfers between devices: 363 us -> 55.8 us
  local copies, waits for them, and re-layouts: 134 us -> 1.36 us
  matrix products: 32.1 us -> 0 us
  starting transfers between devices: 0.04 us -> 21.9 us
  between operations: 14.2 us -> 0.76 us
  Pallas kernels: 0 us -> 12.5 us
  other arithmetic: 13.5 us -> 2.2 us
    reduce_scatter x1 -> x0, waiting for transfers between devices: 363 us -> none  [per_device(): lax.psum_scatter(blocks.reshape(feature_share * BINS * lax.axis_size('row...]
    psum x2 -> x0, blocking collectives: 356 us -> none  [the longest x1 351 us: per_device(): split_sums = lax.psum(local_stats, 'row')]
    pmax x2 -> x0, blocking collectives: 192 us -> none  [the longest x1 185 us: per_device(): best_gain = lax.pmax(local_best, 'row')]
    all_to_all x0 -> x2, waiting for transfers between devices: none -> 54.5 us  [the longest x1 40.6 us: per_device(): taken = lax.all_to_all(send, ROW, 0, 0)]
    slice x4 -> x0, local copies, waits for them, and re-layouts: 36.9 us -> none  [the longest x2 24.5 us: per_device(): grad_left = running[:, :-1, :, :, 0]]
    gather x5 -> x0, local copies, waits for them, and re-layouts: 33.1 us -> none  [per_device(): value_at = jnp.take_along_axis(bins, row_feature, axis=1)]
    dot_general x16 -> x0, matrix products: 32.1 us -> none  [one_group(): lax.dot_general(onehot, paired, (((0,), (0,)), ((), ())), preferred_eleme...]
    reshape x4 -> x1, local copies, waits for them, and re-layouts: 27.4 us -> 0.08 us  [per_device(): lax.dynamic_slice_in_dim(picks, xh * PART, PART, 0)]
  transfers between devices with their start and end apart: 1 -> 3, of which waited for: 1 -> 3; matrix products, arithmetic and copies ran while one was open for 3% -> 0% of each run, Pallas kernels for 0% -> 0%
where the time goes in v1:
time: 101 us; the launch traced here: 99.9 us
  waiting for transfers between devices  55.8 us (55%)
  starting transfers between devices  21.9 us (22%)
  Pallas kernels  12.5 us (12%)
  blocking collectives  5.41 us (5%)
  other arithmetic  2.2 us (2%)
  local copies, waits for them, and re-layouts  1.36 us (1%)
    all_to_all x1, waiting for transfers between devices, per_device(): taken = lax.all_to_all(send, ROW, 0, 0)  40.6 us
    all_to_all x1, starting transfers between devices, per_device(): taken = lax.all_to_all(send, ROW, 0, 0)  14.7 us
    all_to_all x1, waiting for transfers between devices, per_device(): gathered = lax.all_to_all(spread, ROW, 0, 0)  13.9 us
    pallas_call x1, Pallas kernels, per_device(): pl.pallas_call(left_kernel, out_shape=jax.ShapeDtypeStruct((128, FEATS *...  7.92 us
    all_to_all x1, starting transfers between devices, per_device(): gathered = lax.all_to_all(spread, ROW, 0, 0)  7.09 us
    all_gather x1, blocking collectives, per_device(): lax.all_gather(jnp.concatenate([scores_t, nodes_t.astype(f32)], axis=0),...  5.41 us
  transfers between devices with their start and end apart: 3, of which 3 were waited for; matrix products, arithmetic and copies ran while one was open for 0% of the time, Pallas kernels for 0%

profile of v1, /device:TPU:8, one launch (start us, length us, event | category | flops | bytes accessed | tf_op | source)
XLA Modules:
  0.0 99.9 jit_solution(2776743765620255108)
XLA Ops:
  0.6 0.7 bitcast_convert_fusion
  1.4 0.7 pad_maximum_fusion
  2.1 5.4 %all-gather = f32[128,256]{1,0:T(8,128)S(1)} all-gather(f32[32,256]{1,0:T(8,128)S(1)} %pad_maximum_fusion), channel_id=2, replica_groups=mesh['xl'=2,'core'=2,'xh'=2,'z'=8,'y'=4] {'xl','core'}, dimensions={0}, use_global_device_ids=true | all-gather | bytes 163840 | tf_op jit(solution)/shard_map/all_gather | solution.py:181
  7.5 0.7 convert_element_type.7
  8.2 0.1 pad_add_fusion.place
  8.2 0.0 copy-start
  8.3 0.9 copy-done
  9.2 1.8 %prepare.1 = f32[64,48,128]{2,1,0:T(8,128)} custom-call(s32[4]{0:T(128)S(1)} %pad_add_fusion.place, f32[4,32,256]{2,1,0:T(8,128)S(1)} %bitcast.19, f32[1,256]{1,0:T(1,128)S(1)} %bitcast.23, s32[256,256]{1,0:T(8,128)S(1)} %copy-done), custom_call_target="tpu_custom_call" | custom-call | tf_op jit(solution)/shard_map/prepare/pallas_call | solution.py:182
  11.0 0.0 copy-start.4
  11.1 0.0 copy-start.5
  11.1 14.7 %all-to-all-start = ((f32[64,48,128]{2,1,0:T(8,128)}), f32[64,48,128]{2,1,0:T(8,128)S(1)}, u32[]{:S(2)}, u32[]{:S(2)}) async-start(f32[64,48,128]{2,1,0:T(8,128)} %prepare.1), calls=%async_computation | async-start | bytes 3145728 | tf_op jit(solution)/shard_map/all_to_all | solution.py:198
  25.8 0.0 copy-done.4
  25.8 0.1 copy.12
  25.9 0.0 copy-done.5
  25.9 0.1 copy.14
  25.9 40.6 %all-to-all-done.taken = f32[64,48,128]{2,1,0:T(8,128)S(1)} async-done(((f32[64,48,128]{2,1,0:T(8,128)}), f32[64,48,128]{2,1,0:T(8,128)S(1)}, u32[]{:S(2)}, u32[]{:S(2)}) %all-to-all-start) | async-done | bytes 1572896 | tf_op jit(solution)/shard_map/all_to_all | solution.py:198
  66.5 7.9 %left.1 = f32[128,1024]{1,0:T(8,128)S(1)} custom-call(s32[4]{0:T(128)S(1)} %pad_add_fusion.place, f32[64,48,128]{2,1,0:T(8,128)S(1)} %all-to-all-done.taken), custom_call_target="tpu_custom_call" | custom-call | tf_op jit(solution)/shard_map/left/pallas_call | solution.py:199
  74.5 0.0 copy-start.1
  74.5 0.0 copy-start.2
  74.5 0.0 copy-start.3
  74.5 0.1 collective-permute-start
  74.7 0.1 copy.15
  74.8 0.1 reshape.13.target
  74.8 1.3 %collective-permute-done.other = f32[64,1024]{1,0:T(8,128)S(1)} collective-permute-done((f32[64,1024]{1,0:T(8,128)S(1)}, f32[64,1024]{1,0:T(8,128)S(1)}, u32[]{:S(2)}, u32[]{:S(2)}) %collective-permute-start) | collective-permute-done | bytes 262176 | tf_op jit(solution)/shard_map/ppermute | solution.py:214
  76.2 1.6 %gain.1 = f32[64,8,128]{2,1,0:T(8,128)} custom-call(s32[4]{0:T(128)S(1)} %pad_add_fusion.place, f32[64,1024]{1,0:T(8,128)S(1)} %get-tuple-element.7.own, f32[64,1024]{1,0:T(8,128)S(1)} %collective-permute-done.other, s32[32,1]{1,0:T(8,128)S(1)} %reshape.13.target), custom_call_target="tpu_custom_call" | custom-call | tf_op jit(solution)/shard_map/gain/pallas_call | solution.py:216
  77.8 7.1 %all-to-all-start.1 = ((f32[64,8,128]{2,1,0:T(8,128)}), f32[64,8,128]{2,1,0:T(8,128)S(1)}, u32[]{:S(2)}, u32[]{:S(2)}) async-start(f32[64,8,128]{2,1,0:T(8,128)} %gain.1), calls=%async_computation.1 | async-start | bytes 524288 | tf_op jit(solution)/shard_map/all_to_all | solution.py:224
  84.9 0.0 copy-done.1
  84.9 0.0 copy-done.2
  84.9 0.3 route.1
  85.2 13.9 %all-to-all-done.1.gathered = f32[64,8,128]{2,1,0:T(8,128)S(1)} async-done(((f32[64,8,128]{2,1,0:T(8,128)}), f32[64,8,128]{2,1,0:T(8,128)S(1)}, u32[]{:S(2)}, u32[]{:S(2)}) %all-to-all-start.1) | async-done | bytes 262176 | tf_op jit(solution)/shard_map/all_to_all | solution.py:224
  99.1 0.0 copy-done.3
  99.1 0.9 finish.1
  (3 shorter events, 0.1 us)
Async XLA Ops:
  8.2 1.0 copy-start
  11.0 14.7 %copy-start.4 = (s32[16,4]{0,1:T(4,128)S(1)}, s32[16,4]{0,1:T(4,128)}, u32[]{:S(2)}) copy-start(s32[16,4]{0,1:T(4,128)} %param.10) | copy-start | bytes 772
  11.1 14.8 %copy-start.5 = (s32[16,4]{0,1:T(4,128)S(1)}, s32[16,4]{0,1:T(4,128)}, u32[]{:S(2)}) copy-start(s32[16,4]{0,1:T(4,128)} %param.11) | copy-start | bytes 772
  11.1 55.5 %all-to-all-start = ((f32[64,48,128]{2,1,0:T(8,128)}), f32[64,48,128]{2,1,0:T(8,128)S(1)}, u32[]{:S(2)}, u32[]{:S(2)}) async-start(f32[64,48,128]{2,1,0:T(8,128)} %prepare.1), calls=%async_computation | async-start | bytes 3145728 | tf_op jit(solution)/shard_map/all_to_all | solution.py:198
  74.5 10.4 %copy-start.1 = (s32[256,256]{1,0:T(8,128)S(1)}, s32[256,256]{1,0:T(8,128)}, u32[]{:S(2)}) copy-start(s32[256,256]{1,0:T(8,128)} %bins.3) | copy-start | bytes 786436
  74.5 10.4 %copy-start.2 = (s32[256,16]{0,1:T(8,128)S(1)}, s32[256,16]{0,1:T(8,128)}, u32[]{:S(2)}) copy-start(s32[256,16]{0,1:T(8,128)} %param.8) | copy-start | bytes 49156
  74.5 24.6 %copy-start.3 = (f32[256,16]{0,1:T(8,128)S(1)}, f32[256,16]{0,1:T(8,128)}, u32[]{:S(2)}) copy-start(f32[256,16]{0,1:T(8,128)} %param.6) | copy-start | bytes 49156
  74.5 1.6 %collective-permute-start = (f32[64,1024]{1,0:T(8,128)S(1)}, f32[64,1024]{1,0:T(8,128)S(1)}, u32[]{:S(2)}, u32[]{:S(2)}) collective-permute-start(f32[64,1024]{1,0:T(8,128)S(1)} %get-tuple-element.6), channel_id=1, source_target_pairs={{0,64},{64,0},{1,65},{65,1},{2,66},{66,2},{3,67},{67,3},{4,68},{68... | collective-permute-start | bytes 786440 | tf_op jit(solution)/shard_map/ppermute | solution.py:214
  77.8 21.3 %all-to-all-start.1 = ((f32[64,8,128]{2,1,0:T(8,128)}), f32[64,8,128]{2,1,0:T(8,128)S(1)}, u32[]{:S(2)}, u32[]{:S(2)}) async-start(f32[64,8,128]{2,1,0:T(8,128)} %gain.1), calls=%async_computation.1 | async-start | bytes 524288 | tf_op jit(solution)/shard_map/all_to_all | solution.py:224

commit v2 on v0

v2 whole, which is shorter than its diff:
```python
import jax
import jax.numpy as jnp
from jax import lax
from jax.experimental import pallas as pl
from jax.experimental.pallas import tpu as pltpu
from jax.sharding import Mesh, PartitionSpec as P

BINS = 128
NODES = 4
SHARD = 16
HALF = 128
PART = 8
FEATS = 8
LAYERS = 8
COLUMNS = 4
BLOCK = 4 * PART + FEATS
PEERS = 2 * COLUMNS

reg_lambda = 1.0
learn_rate = 0.5

CLS = ("xl", "core")
ROW = ("xh", "z", "y")
VMEM = pl.BlockSpec(memory_space=pltpu.VMEM)
SMEM = pl.BlockSpec(memory_space=pltpu.SMEM)
BF16 = jnp.bfloat16
F32 = jnp.float32
LAST_DIMS = (((1,), (1,)), ((), ()))


def params(mib):
    return pltpu.CompilerParams(vmem_limit_bytes=mib * 1024 * 1024)


def call(kernel, name, shapes, specs, args, scratch=(), mib=16):
    many = isinstance(shapes, tuple)
    return pl.pallas_call(
        kernel,
        out_shape=shapes,
        in_specs=specs,
        out_specs=(VMEM,) * len(shapes) if many else VMEM,
        scratch_shapes=list(scratch),
        compiler_params=params(mib),
        name=name,
    )(*args)


def join_kernel(scores, nodes, joined):
    joined[:SHARD] = scores[...]
    joined[SHARD:] = nodes[...].astype(F32)


def prepare_kernel(place, every, labels, bins, send, columns, sem):
    xl, core = place[0], place[1]
    start = pl.multiple_of(core * HALF, HALF)
    fetch = pltpu.make_async_copy(bins.at[pl.ds(start, HALF), :], columns, sem)
    fetch.start()

    def half(x):
        return jnp.where(core == 0, x[..., :HALF], x[..., HALF:])

    scores = [half(every[i, :SHARD, :]) for i in range(4)]
    nodes = [half(every[i, SHARD:, :]) for i in range(4)]
    label = half(labels[...]).astype(F32)
    top = jnp.max(jnp.maximum(jnp.maximum(scores[0], scores[1]), jnp.maximum(scores[2], scores[3])), axis=0, keepdims=True)
    exponent = [jnp.exp(s - top) for s in scores]
    denominator = jnp.sum((exponent[0] + exponent[1]) + (exponent[2] + exponent[3]), axis=0, keepdims=True)
    label_rows = jnp.broadcast_to(label, (8, HALF))
    common = []
    for i in range(2):
        common.append(jnp.where(xl == 0, exponent[i], exponent[2 + i]) / denominator)
    for i in range(2):
        common.append(jnp.where(xl == 0, nodes[i], nodes[2 + i]))
    for layer in range(LAYERS):
        for i in range(4):
            send[layer, i * SHARD : (i + 1) * SHARD] = common[i]
        send[layer, 96:104] = label_rows
    fetch.wait()
    turned = columns[...].astype(F32).T
    width = COLUMNS * FEATS
    for layer in range(LAYERS):
        send[layer, 64:96] = turned[layer * width : (layer + 1) * width]


def relay_kernel(came, send):
    for layer in range(LAYERS):
        for q in range(2):
            parts = [came[layer, i * SHARD + q * PART : i * SHARD + (q + 1) * PART] for i in range(4)]
            for y in range(COLUMNS):
                for i in range(4):
                    row = layer * BLOCK + i * PART
                    send[q * COLUMNS + y, row : row + PART] = parts[i]
        for y in range(COLUMNS):
            columns = came[layer, 64 + y * FEATS : 64 + (y + 1) * FEATS]
            for q in range(2):
                row = layer * BLOCK + 4 * PART
                send[q * COLUMNS + y, row : row + FEATS] = columns
    labels = jnp.concatenate([came[layer, 96:97] for layer in range(LAYERS)], axis=0)
    for peer in range(PEERS):
        send[peer, LAYERS * BLOCK :] = labels


def route_kernel(picks, nodes, bins, route):
    pick = picks[...]
    column = jnp.concatenate([pick[:, n : n + 1] for n in range(NODES)], axis=0)
    features = bins.shape[1]
    hot = (lax.broadcasted_iota(jnp.int32, (NODES * SHARD, features), 1) == (column // BINS)).astype(BF16)
    value = lax.dot_general(hot, bins[...].astype(BF16), LAST_DIMS, preferred_element_type=F32)
    right = (value > (column % BINS).astype(F32)).astype(jnp.int32)
    node = nodes[...]
    out = 2 * node
    for n in range(NODES):
        out = out + jnp.where(node == n, right[n * SHARD : (n + 1) * SHARD], 0)
    route[...] = out


def left_kernel(place, taken, own, away, left, *buffers):
    xl, core, quarter = place[0], place[1], place[2]
    class_id = lax.broadcasted_iota(jnp.int32, (PART, HALF), 0) + quarter * PART
    ids = [(class_id + (2 * xl + shard) * SHARD).astype(F32) for shard in range(2)]
    bin_range = lax.broadcasted_iota(jnp.int32, (BINS, HALF), 0).astype(BF16)
    one, zero = jnp.ones((), BF16), jnp.zeros((), BF16)

    def build(source, paired, mask):
        for layer in range(LAYERS):
            lanes = slice(layer * HALF, (layer + 1) * HALF)
            base = layer * BLOCK
            label = jnp.broadcast_to(taken[source, LAYERS * BLOCK + layer : LAYERS * BLOCK + layer + 1], (PART, HALF))
            tiles = []
            for shard in range(2):
                prob = taken[source, base + shard * PART : base + (shard + 1) * PART]
                node = taken[source, base + (2 + shard) * PART : base + (3 + shard) * PART]
                target = (label == ids[shard]).astype(F32)
                for value in (prob - target, 2.0 * prob * (1.0 - prob)):
                    tiles += [jnp.where(node == float(n), value, 0.0) for n in range(NODES)]
            paired[:, lanes] = jnp.concatenate(tiles, axis=0).astype(BF16)
            for f in range(FEATS):
                row = taken[source, base + 4 * PART + f : base + 4 * PART + f + 1]
                row = jnp.broadcast_to(row, (BINS, HALF)).astype(BF16)
                mask[f * BINS : (f + 1) * BINS, lanes] = jnp.where(bin_range >= row, one, zero)

    def multiply(paired, mask):
        left[...] += lax.dot_general(mask[...], paired[...], LAST_DIMS, preferred_element_type=F32)

    even, odd = buffers[:2], buffers[2:]
    left[...] = jnp.zeros_like(left)
    build(0, *even)

    @pl.loop(0, PEERS // 2)
    def _(pair):
        build(2 * pair + 1, *odd)
        multiply(*even)
        build(jnp.minimum(2 * pair + 2, PEERS - 1), *even)
        multiply(*odd)

    middle = FEATS * BINS // 2
    low = lax.broadcasted_iota(jnp.int32, (BINS, 128), 1) < 64
    for row in range(0, middle, BINS):
        a, b = left[row : row + BINS], left[middle + row : middle + row + BINS]
        first = jnp.where(low, a, pltpu.roll(b, 64, 1))
        second = jnp.where(low, pltpu.roll(a, 64, 1), b)
        own[row : row + BINS] = jnp.where(core == 0, first, second)
        away[row : row + BINS] = jnp.where(core == 0, second, first)


def gain_kernel(place, own, other, target, spread):
    group = place[3]
    lane = lax.broadcasted_iota(jnp.int32, (1, 128), 1)
    pick = target[...] - group * (FEATS * BINS) - jnp.where(lane >= 64, FEATS * BINS // 2, 0)
    line = lax.broadcasted_iota(jnp.int32, (BINS, 128), 0)
    best = jnp.full((BINS, 128), -jnp.inf, F32)
    sums = jnp.zeros((BINS, 128), F32)
    totals = jnp.zeros((1, 128), F32)
    for f in range(FEATS // 2):
        rows = slice(f * BINS, (f + 1) * BINS)
        g = own[rows] + other[rows]
        h = pltpu.roll(g, 96, 1)
        gt, ht = g[BINS - 1 :], h[BINS - 1 :]
        gain = 0.5 * (g * g / (h + reg_lambda) + (gt - g) ** 2 / (ht - h + reg_lambda) - gt * gt / (ht + reg_lambda))
        best = jnp.maximum(best, jnp.where(line == BINS - 1, -jnp.inf, gain))
        sums = jnp.where(line + f * BINS == pick, g, sums)
        inside = (pick >= f * BINS) & (pick < (f + 1) * BINS)
        totals = jnp.where(inside, gt, totals)
    best = jnp.max(best, axis=0, keepdims=True)
    sums = jnp.sum(sums, axis=0, keepdims=True)
    best = jnp.maximum(best, pltpu.roll(best, 64, 1))
    sums = sums + pltpu.roll(sums, 64, 1)
    totals = totals + pltpu.roll(totals, 64, 1)
    block = jnp.concatenate([best, jnp.where(lane < 64, sums, totals)], axis=0)
    for chip in range(spread.shape[0]):
        spread[chip] = block


def finish_kernel(gathered, scores, route, best, new_scores):
    chips = gathered.shape[0]
    weights = []
    for q in range(2):
        blocks = [gathered[chip] for chip in range(q * chips // 2, (q + 1) * chips // 2)]
        top, total = blocks[0], blocks[0]
        for block in blocks[1:]:
            top = jnp.maximum(top, block)
            total = total + block
        for n in range(NODES):
            best[n : n + 1, q * PART : (q + 1) * PART] = top[0:1, n * PART : (n + 1) * PART]
        total = total[1:2]
        gl = total
        hl, gt, ht = (pltpu.roll(total, 128 - 32 * j, 1) for j in (1, 2, 3))
        weights.append(-gl / (hl + reg_lambda))
        weights.append(-(gt - gl) / (ht - hl + reg_lambda))
    columns = jnp.concatenate(weights + [jnp.zeros((4, 128), F32)], axis=0).T
    way = route[...]
    for q in range(2):
        part = slice(q * PART, (q + 1) * PART)
        leaf = jnp.zeros((PART, way.shape[1]), F32)
        for n in range(NODES):
            for side in range(2):
                value = columns[n * PART : (n + 1) * PART, 2 * q + side : 2 * q + side + 1]
                leaf = jnp.where(way[part] == 2 * n + side, value, leaf)
        new_scores[part] = scores[part] + learn_rate * leaf


def per_device(scores, labels, nodes, bins, pick_feature, pick_bin):
    xl, core, xh = (lax.axis_index(a) for a in ("xl", "core", "xh"))
    group = lax.axis_index("z") * COLUMNS + lax.axis_index("y")
    place = jnp.stack([xl, core, xh, group]).astype(jnp.int32)
    rows = 2 * HALF
    chips = PEERS * LAYERS
    scores_t, nodes_t = scores.T, nodes.T
    shape = lambda *s: jax.ShapeDtypeStruct(s, F32)

    joined = call(join_kernel, "join", shape(2 * SHARD, rows), [VMEM] * 2, (scores_t, nodes_t))
    every = lax.all_gather(joined, CLS)
    send = call(
        prepare_kernel, "prepare", shape(LAYERS, 104, HALF), [SMEM, VMEM, VMEM, pl.BlockSpec(memory_space=pltpu.HBM)],
        (place, every, labels[None], bins),
        scratch=[pltpu.VMEM((HALF, bins.shape[1]), jnp.int32), pltpu.SemaphoreType.DMA],
    )
    came = lax.all_to_all(send, "z", 0, 0)
    send = call(relay_kernel, "relay", shape(PEERS, LAYERS * (BLOCK + 1), HALF), [VMEM], (came,))
    taken = lax.all_to_all(send, ("xh", "y"), 0, 0)
    picks = pick_feature * BINS + pick_bin
    route = call(
        route_kernel, "route", jax.ShapeDtypeStruct((SHARD, rows), jnp.int32), [VMEM] * 3, (picks, nodes_t, bins)
    )
    target = lax.dynamic_slice_in_dim(picks, xh * PART, PART, 0).T.reshape(1, NODES * PART)
    target = jnp.tile(target, (1, 4))
    buffer = [pltpu.VMEM((128, LAYERS * HALF), BF16), pltpu.VMEM((FEATS * BINS, LAYERS * HALF), BF16)]
    half = shape(FEATS * BINS // 2, 128)
    own, away = call(
        left_kernel, "left", (half, half), [SMEM, VMEM], (place, taken),
        scratch=[pltpu.VMEM((FEATS * BINS, 128), F32)] + buffer + buffer, mib=32,
    )
    other = lax.ppermute(away, "core", [(0, 1), (1, 0)])
    spread = call(gain_kernel, "gain", shape(chips, 2, 128), [SMEM, VMEM, VMEM, VMEM], (place, own, other, target))
    gathered = lax.all_to_all(spread, ROW, 0, 0)
    best, new_scores = call(
        finish_kernel, "finish", (shape(NODES, SHARD), shape(SHARD, rows)), [VMEM] * 3, (gathered, scores_t, route)
    )
    return best.T, new_scores.T


def solution(mesh):
    fine = Mesh(mesh.devices.reshape(2, 2, 2, LAYERS, COLUMNS), CLS + ROW)
    in_specs = (P(ROW, CLS), P(ROW), P(ROW, CLS), P(ROW, None), P(CLS, None), P(CLS, None))
    out_specs = (P(CLS, None), P(ROW, CLS))
    return jax.shard_map(per_device, mesh=fine, in_specs=in_specs, out_specs=out_specs, check_vma=False)
```

time: 1120 us -> 89.8 us (0.08)
  blocking collectives: 548 us -> 29.6 us
  waiting for transfers between devices: 363 us -> 29.8 us
  local copies, waits for them, and re-layouts: 134 us -> 3.51 us
  matrix products: 32.1 us -> 0 us
  starting transfers between devices: 0.04 us -> 13.5 us
  between operations: 14.2 us -> 0.75 us
  other arithmetic: 13.5 us -> 0.08 us
  Pallas kernels: 0 us -> 11.4 us
    reduce_scatter x1 -> x0, waiting for transfers between devices: 363 us -> none  [per_device(): lax.psum_scatter(blocks.reshape(feature_share * BINS * lax.axis_size('row...]
    psum x2 -> x0, blocking collectives: 356 us -> none  [the longest x1 351 us: per_device(): split_sums = lax.psum(local_stats, 'row')]
    pmax x2 -> x0, blocking collectives: 192 us -> none  [the longest x1 185 us: per_device(): best_gain = lax.pmax(local_best, 'row')]
    slice x4 -> x0, local copies, waits for them, and re-layouts: 36.9 us -> none  [the longest x2 24.5 us: per_device(): grad_left = running[:, :-1, :, :, 0]]
    gather x5 -> x0, local copies, waits for them, and re-layouts: 33.1 us -> none  [per_device(): value_at = jnp.take_along_axis(bins, row_feature, axis=1)]
    dot_general x16 -> x0, matrix products: 32.1 us -> none  [one_group(): lax.dot_general(onehot, paired, (((0,), (0,)), ((), ())), preferred_eleme...]
    all_to_all x0 -> x2, waiting for transfers between devices: none -> 28.6 us  [the longest x1 17.6 us: per_device(): taken = lax.all_to_all(send, ('xh', 'y'), 0, 0)]
    reshape x4 -> x0, local copies, waits for them, and re-layouts: 27.4 us -> none  [the longest x1 17.4 us: per_device(): blocks.reshape(feature_share * BINS * lax.axis_size('row'), column_count)]
  transfers between devices with their start and end apart: 1 -> 3, of which waited for: 1 -> 3; matrix products, arithmetic and copies ran while one was open for 3% -> 0% of each run, Pallas kernels for 0% -> 0%
where the time goes in v2:
time: 89.8 us; the launch traced here: 88.6 us
  waiting for transfers between devices  29.8 us (33%)
  blocking collectives  29.6 us (33%)
  starting transfers between devices  13.5 us (15%)
  Pallas kernels  11.4 us (13%)
  local copies, waits for them, and re-layouts  3.51 us (4%)
    all_to_all x1, blocking collectives, per_device(): came = lax.all_to_all(send, 'z', 0, 0)  24.2 us
    all_to_all x1, waiting for transfers between devices, per_device(): taken = lax.all_to_all(send, ('xh', 'y'), 0, 0)  17.6 us
    pallas_call x7, Pallas kernels, call(): pl.pallas_call(kernel, out_shape=shapes, in_specs=specs, out_specs=(VMEM,...  11.4 us
    all_to_all x1, waiting for transfers between devices, per_device(): gathered = lax.all_to_all(spread, ROW, 0, 0)  11 us
    all_to_all x1, starting transfers between devices, per_device(): taken = lax.all_to_all(send, ('xh', 'y'), 0, 0)  7.51 us
    all_to_all x1, starting transfers between devices, per_device(): gathered = lax.all_to_all(spread, ROW, 0, 0)  5.92 us
    all_gather x1, blocking collectives, per_device(): every = lax.all_gather(joined, CLS)  5.41 us
    unnamed x20, local copies, waits for them, and re-layouts  3.24 us
  transfers between devices with their start and end apart: 3, of which 3 were waited for; matrix products, arithmetic and copies ran while one was open for 0% of the time, Pallas kernels for 0%

profile of v2, /device:TPU:8, one launch (start us, length us, event | category | flops | bytes accessed | tf_op | source)
XLA Modules:
  0.0 88.6 jit_solution(6405470695428558313)
XLA Ops:
  0.6 0.0 copy-start.2
  0.6 0.7 copy-done.2
  1.4 0.0 copy-start.4
  1.4 0.7 copy-done.4
  2.1 5.4 %all-gather = f32[128,256]{1,0:T(8,128)S(1)} all-gather(f32[32,256]{1,0:T(8,128)S(1)} %join.1), channel_id=2, replica_groups=mesh['xl'=2,'core'=2,'xh'=2,'z'=8,'y'=4] {'xl','core'}, dimensions={0}, use_global_device_ids=true | all-gather | bytes 163840 | tf_op jit(solution)/shard_map/all_gather | solution.py:232
  7.5 0.1 pad_add_fusion.place
  7.6 0.0 copy-start
  7.6 0.9 %copy-done = s32[256,256]{1,0:T(8,128)S(1)} copy-done((s32[256,256]{1,0:T(8,128)S(1)}, s32[256,256]{1,0:T(8,128)}, u32[]{:S(2)}) %copy-start) | copy-done | bytes 262168
  8.5 0.0 copy-start.6
  8.5 0.7 copy-done.6
  9.2 0.9 prepare.1
  10.1 24.2 %all_to_all.15.came = f32[8,104,128]{2,1,0:T(8,128)S(1)} all-to-all(f32[8,104,128]{2,1,0:T(8,128)S(1)} %prepare.1), channel_id=1, replica_groups=mesh['xl'=2,'core'=2,'xh'=2,'z'=8,'y'=4] {'z'}, dimensions={0} | all-to-all | bytes 851968 | tf_op jit(solution)/shard_map/all_to_all | solution.py:238
  34.2 1.2 %relay.1 = f32[8,328,128]{2,1,0:T(8,128)} custom-call(f32[8,104,128]{2,1,0:T(8,128)S(1)} %all_to_all.15.came), custom_call_target="tpu_custom_call" | custom-call | tf_op jit(solution)/shard_map/relay/pallas_call | solution.py:37
  35.4 0.0 copy-start.7
  35.4 0.0 copy-start.8
  35.4 7.5 %all-to-all-start.1 = ((f32[8,328,128]{2,1,0:T(8,128)}), f32[8,328,128]{2,1,0:T(8,128)S(1)}, u32[]{:S(2)}, u32[]{:S(2)}) async-start(f32[8,328,128]{2,1,0:T(8,128)} %relay.1), calls=%async_computation.1 | async-start | bytes 2686976 | tf_op jit(solution)/shard_map/all_to_all | solution.py:240
  42.9 0.0 copy-start.1
  42.9 0.0 copy-start.3
  42.9 0.0 copy-start.5
  42.9 0.0 copy-done.7
  43.0 0.1 copy.11
  43.0 0.0 copy-done.8
  43.0 0.1 copy.13
  43.1 17.6 %all-to-all-done.1.taken = f32[8,328,128]{2,1,0:T(8,128)S(1)} async-done(((f32[8,328,128]{2,1,0:T(8,128)}), f32[8,328,128]{2,1,0:T(8,128)S(1)}, u32[]{:S(2)}, u32[]{:S(2)}) %all-to-all-start.1) | async-done | bytes 1343520 | tf_op jit(solution)/shard_map/all_to_all | solution.py:240
  60.8 6.7 %left.1 = (f32[512,128]{1,0:T(8,128)S(1)}, f32[512,128]{1,0:T(8,128)S(1)}) custom-call(s32[4]{0:T(128)S(1)} %pad_add_fusion.place, f32[8,328,128]{2,1,0:T(8,128)S(1)} %all-to-all-done.1.taken), custom_call_target="tpu_custom_call" | custom-call | tf_op jit(solution)/shard_map/left/pallas_call | solution.py:37
  67.5 0.1 collective-permute-start
  67.6 0.1 copy.14
  67.7 0.1 tile.10
  67.8 0.1 tile.12.target
  67.9 1.2 %collective-permute-done.other = f32[512,128]{1,0:T(8,128)S(1)} collective-permute-done((f32[512,128]{1,0:T(8,128)S(1)}, f32[512,128]{1,0:T(8,128)S(1)}, u32[]{:S(2)}, u32[]{:S(2)}) %collective-permute-start) | collective-permute-done | bytes 262176 | tf_op jit(solution)/shard_map/ppermute | solution.py:253
  69.1 1.4 %gain.1 = f32[64,2,128]{2,1,0:T(2,128)} custom-call(s32[4]{0:T(128)S(1)} %pad_add_fusion.place, f32[512,128]{1,0:T(8,128)S(1)} %get-tuple-element.6.own, f32[512,128]{1,0:T(8,128)S(1)} %collective-permute-done.other, s32[1,128]{1,0:T(1,128)S(1)} %tile.12.target), custom_call_target="tpu_custom_call" | custom-call | tf_op jit(solution)/shard_map/gain/pallas_call | solution.py:37
  70.5 5.9 %all-to-all-start.2 = ((f32[64,2,128]{2,1,0:T(2,128)}), f32[64,2,128]{2,1,0:T(2,128)S(1)}, u32[]{:S(2)}, u32[]{:S(2)}) async-start(f32[64,2,128]{2,1,0:T(2,128)} %gain.1), calls=%async_computation.2 | async-start | bytes 131072 | tf_op jit(solution)/shard_map/all_to_all | solution.py:255
  76.5 0.0 copy-done.1
  76.5 0.0 copy-done.3
  76.5 0.3 route.1
  76.8 11.0 %all-to-all-done.2.gathered = f32[64,2,128]{2,1,0:T(2,128)S(1)} async-done(((f32[64,2,128]{2,1,0:T(2,128)}), f32[64,2,128]{2,1,0:T(2,128)S(1)}, u32[]{:S(2)}, u32[]{:S(2)}) %all-to-all-start.2) | async-done | bytes 65568 | tf_op jit(solution)/shard_map/all_to_all | solution.py:255
  87.7 0.0 copy-done.5
  87.7 0.9 %finish.1 = (f32[4,16]{1,0:T(4,128)}, f32[16,256]{1,0:T(8,128)}) custom-call(f32[64,2,128]{2,1,0:T(2,128)S(1)} %all-to-all-done.2.gathered, f32[16,256]{1,0:T(8,128)S(1)} %bitcast.16, s32[16,256]{1,0:T(8,128)S(1)} %route.1), custom_call_target="tpu_custom_call" | custom-call | tf_op jit(solution)/shard_map/finish/pallas_call | solution.py:37
  (4 shorter events, 0.0 us)
Async XLA Ops:
  0.6 0.7 copy-start.2
  1.4 0.7 copy-start.4
  7.6 1.0 %copy-start = (s32[256,256]{1,0:T(8,128)S(1)}, s32[256,256]{1,0:T(8,128)}, u32[]{:S(2)}) copy-start(s32[256,256]{1,0:T(8,128)} %bins.3) | copy-start | bytes 786436
  8.5 0.7 copy-start.6
  35.4 7.5 %copy-start.7 = (s32[16,4]{0,1:T(4,128)S(1)}, s32[16,4]{0,1:T(4,128)}, u32[]{:S(2)}) copy-start(s32[16,4]{0,1:T(4,128)} %param.10) | copy-start | bytes 772
  35.4 7.6 %copy-start.8 = (s32[16,4]{0,1:T(4,128)S(1)}, s32[16,4]{0,1:T(4,128)}, u32[]{:S(2)}) copy-start(s32[16,4]{0,1:T(4,128)} %param.11) | copy-start | bytes 772
  35.4 25.4 %all-to-all-start.1 = ((f32[8,328,128]{2,1,0:T(8,128)}), f32[8,328,128]{2,1,0:T(8,128)S(1)}, u32[]{:S(2)}, u32[]{:S(2)}) async-start(f32[8,328,128]{2,1,0:T(8,128)} %relay.1), calls=%async_computation.1 | async-start | bytes 2686976 | tf_op jit(solution)/shard_map/all_to_all | solution.py:240
  42.9 33.5 %copy-start.1 = (s32[256,256]{1,0:T(8,128)S(1)}, s32[256,256]{1,0:T(8,128)}, u32[]{:S(2)}) copy-start(s32[256,256]{1,0:T(8,128)} %bins.3) | copy-start | bytes 786436
  42.9 33.5 %copy-start.3 = (s32[256,16]{0,1:T(8,128)S(1)}, s32[256,16]{0,1:T(8,128)}, u32[]{:S(2)}) copy-start(s32[256,16]{0,1:T(8,128)} %param.8) | copy-start | bytes 49156
  42.9 44.8 %copy-start.5 = (f32[256,16]{0,1:T(8,128)S(1)}, f32[256,16]{0,1:T(8,128)}, u32[]{:S(2)}) copy-start(f32[256,16]{0,1:T(8,128)} %param.6) | copy-start | bytes 49156
  67.5 1.6 %collective-permute-start = (f32[512,128]{1,0:T(8,128)S(1)}, f32[512,128]{1,0:T(8,128)S(1)}, u32[]{:S(2)}, u32[]{:S(2)}) collective-permute-start(f32[512,128]{1,0:T(8,128)S(1)} %get-tuple-element.7), channel_id=1, source_target_pairs={{0,64},{64,0},{1,65},{65,1},{2,66},{66,2},{3,67},{67,3},{4,68},{68... | collective-permute-start | bytes 786440 | tf_op jit(solution)/shard_map/ppermute | solution.py:253
  70.5 17.2 %all-to-all-start.2 = ((f32[64,2,128]{2,1,0:T(2,128)}), f32[64,2,128]{2,1,0:T(2,128)S(1)}, u32[]{:S(2)}, u32[]{:S(2)}) async-start(f32[64,2,128]{2,1,0:T(2,128)} %gain.1), calls=%async_computation.2 | async-start | bytes 131072 | tf_op jit(solution)/shard_map/all_to_all | solution.py:255

commit v3 on v2

--- a/solution.py
+++ b/solution.py
@@ -22,9 +22,11 @@
 CLS = ("xl", "core")
 ROW = ("xh", "z", "y")
 VMEM = pl.BlockSpec(memory_space=pltpu.VMEM)
+HBM = pl.BlockSpec(memory_space=pltpu.HBM)
 SMEM = pl.BlockSpec(memory_space=pltpu.SMEM)
 BF16 = jnp.bfloat16
 F32 = jnp.float32
+PIN = lambda x: pltpu.with_memory_space_constraint(x, pltpu.HBM)
 LAST_DIMS = (((1,), (1,)), ((), ()))
 
 
@@ -45,41 +47,44 @@
     )(*args)
 
 
-def join_kernel(scores, nodes, joined):
-    joined[:SHARD] = scores[...]
-    joined[SHARD:] = nodes[...].astype(F32)
-
-
-def prepare_kernel(place, every, labels, bins, send, columns, sem):
-    xl, core = place[0], place[1]
+def join_kernel(scores, nodes, labels, bins, joined, turned, label, node_buffer, label_buffer, columns, sems):
+    core = lax.axis_index("core")
     start = pl.multiple_of(core * HALF, HALF)
-    fetch = pltpu.make_async_copy(bins.at[pl.ds(start, HALF), :], columns, sem)
-    fetch.start()
+    copies = [
+        pltpu.make_async_copy(bins.at[pl.ds(start, HALF), :], columns, sems.at[0]),
+        pltpu.make_async_copy(scores, joined.at[pl.ds(0, SHARD), :], sems.at[1]),
+        pltpu.make_async_copy(nodes, node_buffer, sems.at[2]),
+        pltpu.make_async_copy(labels, label_buffer, sems.at[3]),
+    ]
+    for copy in copies:
+        copy.start()
+    for copy in copies:
+        copy.wait()
+    joined[SHARD:] = node_buffer[...].astype(F32)
+    turned[...] = columns[...].astype(F32).T
+    row = label_buffer[...].astype(F32)
+    label[...] = jnp.broadcast_to(jnp.where(core == 0, row[:, :HALF], row[:, HALF:]), label.shape)
+
+
+def prepare_kernel(every, turned, label, send):
+    xl, core = lax.axis_index("xl"), lax.axis_index("core")
 
     def half(x):
         return jnp.where(core == 0, x[..., :HALF], x[..., HALF:])
 
     scores = [half(every[i, :SHARD, :]) for i in range(4)]
     nodes = [half(every[i, SHARD:, :]) for i in range(4)]
-    label = half(labels[...]).astype(F32)
     top = jnp.max(jnp.maximum(jnp.maximum(scores[0], scores[1]), jnp.maximum(scores[2], scores[3])), axis=0, keepdims=True)
     exponent = [jnp.exp(s - top) for s in scores]
     denominator = jnp.sum((exponent[0] + exponent[1]) + (exponent[2] + exponent[3]), axis=0, keepdims=True)
-    label_rows = jnp.broadcast_to(label, (8, HALF))
-    common = []
-    for i in range(2):
-        common.append(jnp.where(xl == 0, exponent[i], exponent[2 + i]) / denominator)
-    for i in range(2):
-        common.append(jnp.where(xl == 0, nodes[i], nodes[2 + i]))
-    for layer in range(LAYERS):
-        for i in range(4):
-            send[layer, i * SHARD : (i + 1) * SHARD] = common[i]
-        send[layer, 96:104] = label_rows
-    fetch.wait()
-    turned = columns[...].astype(F32).T
+    prob = [jnp.where(xl == 0, exponent[i], exponent[2 + i]) / denominator for i in range(2)]
+    node = [jnp.where(xl == 0, nodes[i], nodes[2 + i]) for i in range(2)]
     width = COLUMNS * FEATS
     for layer in range(LAYERS):
+        for i, part in enumerate(prob + node):
+            send[layer, i * SHARD : (i + 1) * SHARD] = part
         send[layer, 64:96] = turned[layer * width : (layer + 1) * width]
+        send[layer, 96:104] = label[...]
 
 
 def relay_kernel(came, send):
@@ -114,8 +119,8 @@
     route[...] = out
 
 
-def left_kernel(place, taken, own, away, left, *buffers):
-    xl, core, quarter = place[0], place[1], place[2]
+def left_kernel(taken, own, away, left, *buffers):
+    xl, core, quarter = (lax.axis_index(a) for a in ("xl", "core", "xh"))
     class_id = lax.broadcasted_iota(jnp.int32, (PART, HALF), 0) + quarter * PART
     ids = [(class_id + (2 * xl + shard) * SHARD).astype(F32) for shard in range(2)]
     bin_range = lax.broadcasted_iota(jnp.int32, (BINS, HALF), 0).astype(BF16)
@@ -163,10 +168,16 @@
         away[row : row + BINS] = jnp.where(core == 0, second, first)
 
 
-def gain_kernel(place, own, other, target, spread):
-    group = place[3]
+def gain_kernel(pick_feature, pick_bin, own, other, spread):
+    quarter = lax.axis_index("xh")
+    group = lax.axis_index("z") * COLUMNS + lax.axis_index("y")
     lane = lax.broadcasted_iota(jnp.int32, (1, 128), 1)
-    pick = target[...] - group * (FEATS * BINS) - jnp.where(lane >= 64, FEATS * BINS // 2, 0)
+    target = jnp.zeros((1, 128), jnp.int32)
+    for n in range(NODES):
+        for k in range(PART):
+            chosen = pick_feature[n, quarter * PART + k] * BINS + pick_bin[n, quarter * PART + k]
+            target = jnp.where(lane % 32 == n * PART + k, chosen, target)
+    pick = target - group * (FEATS * BINS) - jnp.where(lane >= 64, FEATS * BINS // 2, 0)
     line = lax.broadcasted_iota(jnp.int32, (BINS, 128), 0)
     best = jnp.full((BINS, 128), -jnp.inf, F32)
     sums = jnp.zeros((BINS, 128), F32)
@@ -220,38 +231,41 @@
 
 
 def per_device(scores, labels, nodes, bins, pick_feature, pick_bin):
-    xl, core, xh = (lax.axis_index(a) for a in ("xl", "core", "xh"))
-    group = lax.axis_index("z") * COLUMNS + lax.axis_index("y")
-    place = jnp.stack([xl, core, xh, group]).astype(jnp.int32)
     rows = 2 * HALF
     chips = PEERS * LAYERS
     scores_t, nodes_t = scores.T, nodes.T
     shape = lambda *s: jax.ShapeDtypeStruct(s, F32)
 
-    joined = call(join_kernel, "join", shape(2 * SHARD, rows), [VMEM] * 2, (scores_t, nodes_t))
+    inputs = [PIN(x) for x in (scores_t, nodes_t, labels[None], bins)]
+    joined, turned, label = call(
+        join_kernel, "join", (shape(2 * SHARD, rows), shape(bins.shape[1], HALF), shape(8, HALF)), [HBM] * 4, inputs,
+        scratch=[
+            pltpu.VMEM((SHARD, rows), jnp.int32),
+            pltpu.VMEM((1, rows), jnp.int32),
+            pltpu.VMEM((HALF, bins.shape[1]), jnp.int32),
+            pltpu.SemaphoreType.DMA((4,)),
+        ],
+    )
     every = lax.all_gather(joined, CLS)
-    send = call(
-        prepare_kernel, "prepare", shape(LAYERS, 104, HALF), [SMEM, VMEM, VMEM, pl.BlockSpec(memory_space=pltpu.HBM)],
-        (place, every, labels[None], bins),
-        scratch=[pltpu.VMEM((HALF, bins.shape[1]), jnp.int32), pltpu.SemaphoreType.DMA],
-    )
+    send = call(prepare_kernel, "prepare", shape(LAYERS, 104, HALF), [VMEM] * 3, (every, turned, label))
     came = lax.all_to_all(send, "z", 0, 0)
     send = call(relay_kernel, "relay", shape(PEERS, LAYERS * (BLOCK + 1), HALF), [VMEM], (came,))
     taken = lax.all_to_all(send, ("xh", "y"), 0, 0)
+    buffer = [pltpu.VMEM((128, LAYERS * HALF), BF16), pltpu.VMEM((FEATS * BINS, LAYERS * HALF), BF16)]
+    half = shape(FEATS * BINS // 2, 128)
+    own, away = call(
+        left_kernel, "left", (half, half), [VMEM], (taken,),
+        scratch=[pltpu.VMEM((FEATS * BINS, 128), F32)] + buffer + buffer, mib=32,
+    )
+    other = lax.ppermute(away, "core", [(0, 1), (1, 0)])
+    spread = call(
+        gain_kernel, "gain", shape(chips, 2, 128), [SMEM, SMEM, VMEM, VMEM], (pick_feature.T, pick_bin.T, own, other)
+    )
+    pick_feature, pick_bin, spread = lax.optimization_barrier((pick_feature, pick_bin, spread))
     picks = pick_feature * BINS + pick_bin
     route = call(
         route_kernel, "route", jax.ShapeDtypeStruct((SHARD, rows), jnp.int32), [VMEM] * 3, (picks, nodes_t, bins)
     )
-    target = lax.dynamic_slice_in_dim(picks, xh * PART, PART, 0).T.reshape(1, NODES * PART)
-    target = jnp.tile(target, (1, 4))
-    buffer = [pltpu.VMEM((128, LAYERS * HALF), BF16), pltpu.VMEM((FEATS * BINS, LAYERS * HALF), BF16)]
-    half = shape(FEATS * BINS // 2, 128)
-    own, away = call(
-        left_kernel, "left", (half, half), [SMEM, VMEM], (place, taken),
-        scratch=[pltpu.VMEM((FEATS * BINS, 128), F32)] + buffer + buffer, mib=32,
-    )
-    other = lax.ppermute(away, "core", [(0, 1), (1, 0)])
-    spread = call(gain_kernel, "gain", shape(chips, 2, 128), [SMEM, VMEM, VMEM, VMEM], (place, own, other, target))
     gathered = lax.all_to_all(spread, ROW, 0, 0)
     best, new_scores = call(
         finish_kernel, "finish", (shape(NODES, SHARD), shape(SHARD, rows)), [VMEM] * 3, (gathered, scores_t, route)

time: 89.8 us -> 86.3 us (0.961)
  blocking collectives: 29.6 us -> 56 us
  waiting for transfers between devices: 29.8 us -> 12.6 us
  starting transfers between devices: 13.5 us -> 5.56 us
  local copies, waits for them, and re-layouts: 3.51 us -> 0.19 us
  Pallas kernels: 11.4 us -> 10.1 us
    all_to_all x0 -> x1, blocking collectives: none -> 26.4 us  [per_device(): taken = lax.all_to_all(send, ('xh', 'y'), 0, 0)]
    all_to_all x1 -> x0, waiting for transfers between devices: 17.6 us -> none  [per_device(): taken = lax.all_to_all(send, ('xh', 'y'), 0, 0)]
    all_to_all x1 -> x0, starting transfers between devices: 7.51 us -> none  [per_device(): taken = lax.all_to_all(send, ('xh', 'y'), 0, 0)]
    unnamed x20 -> x10, local copies, waits for them, and re-layouts: 3.24 us -> 0.02 us
    pallas_call x7, Pallas kernels: 11.4 us -> 10.1 us  [call(): pl.pallas_call(kernel, out_shape=shapes, in_specs=specs, out_specs=(VMEM,...]
  transfers between devices with their start and end apart: 3 -> 2, of which waited for: 3 -> 2; matrix products, arithmetic and copies ran while one was open for 0% -> 0% of each run, Pallas kernels for 0% -> 0%
where the time goes in v3:
time: 86.3 us; the launch traced here: 85.1 us
  blocking collectives  56 us (65%)
  waiting for transfers between devices  12.6 us (15%)
  Pallas kernels  10.1 us (12%)
  starting transfers between devices  5.56 us (6%)
    all_to_all x1, blocking collectives, per_device(): taken = lax.all_to_all(send, ('xh', 'y'), 0, 0)  26.4 us
    all_to_all x1, blocking collectives, per_device(): came = lax.all_to_all(send, 'z', 0, 0)  24.2 us
    all_to_all x1, waiting for transfers between devices, per_device(): gathered = lax.all_to_all(spread, ROW, 0, 0)  11.1 us
    pallas_call x7, Pallas kernels, call(): pl.pallas_call(kernel, out_shape=shapes, in_specs=specs, out_specs=(VMEM,...  10.1 us
    all_to_all x1, starting transfers between devices, per_device(): gathered = lax.all_to_all(spread, ROW, 0, 0)  5.47 us
    all_gather x1, blocking collectives, per_device(): every = lax.all_gather(joined, CLS)  5.43 us
  transfers between devices with their start and end apart: 2, of which 2 were waited for; matrix products, arithmetic and copies ran while one was open for 0% of the time, Pallas kernels for 0%

profile of v3, /device:TPU:8, one launch (start us, length us, event | category | flops | bytes accessed | tf_op | source)
XLA Modules:
  0.0 85.1 jit_solution(1987943340233483631)
XLA Ops:
  0.6 1.1 %join.1 = (f32[32,256]{1,0:T(8,128)S(1)}, f32[256,128]{1,0:T(8,128)S(1)}, f32[8,128]{1,0:T(8,128)S(1)}) custom-call(f32[16,256]{1,0:T(8,128)} %bitcast.11, s32[16,256]{1,0:T(8,128)} %bitcast.9, s32[1,256]{1,0:T(1,128)} %bitcast.15, s32[256,256]{1,0:T(8,128)} %bins.3), custom_call_target="tpu_custom_call" | custom-call | tf_op jit(solution)/shard_map/join/pallas_call | solution.py:39
  1.7 5.4 %all-gather = f32[128,256]{1,0:T(8,128)S(1)} all-gather(f32[32,256]{1,0:T(8,128)S(1)} %get-tuple-element.12), channel_id=2, replica_groups=mesh['xl'=2,'core'=2,'xh'=2,'z'=8,'y'=4] {'xl','core'}, dimensions={0}, use_global_device_ids=true | all-gather | bytes 163840 | tf_op jit(solution)/shard_map/all_gather | solution.py:249
  7.1 0.1 prepare.1
  7.2 24.2 %all_to_all.15.came = f32[8,104,128]{2,1,0:T(8,128)S(1)} all-to-all(f32[8,104,128]{2,1,0:T(8,128)S(1)} %prepare.1), channel_id=1, replica_groups=mesh['xl'=2,'core'=2,'xh'=2,'z'=8,'y'=4] {'z'}, dimensions={0} | all-to-all | bytes 851968 | tf_op jit(solution)/shard_map/all_to_all | solution.py:251
  31.3 0.1 relay.1
  31.4 26.4 %all_to_all.16.taken = f32[8,328,128]{2,1,0:T(8,128)S(1)} all-to-all(f32[8,328,128]{2,1,0:T(8,128)S(1)} %relay.1), channel_id=1, replica_groups=mesh['xl'=2,'core'=2,'xh'=2,'z'=8,'y'=4] {'xh','y'}, dimensions={0} | all-to-all | bytes 2686976 | tf_op jit(solution)/shard_map/all_to_all | solution.py:253
  57.8 0.0 copy-start.3
  57.8 0.0 copy-start.4
  57.8 0.0 copy-start
  57.8 0.0 copy-start.1
  57.8 0.0 copy-start.2
  57.8 6.2 %left.1 = (f32[512,128]{1,0:T(8,128)S(1)}, f32[512,128]{1,0:T(8,128)S(1)}) custom-call(f32[8,328,128]{2,1,0:T(8,128)S(1)} %all_to_all.16.taken), custom_call_target="tpu_custom_call" | custom-call | tf_op jit(solution)/shard_map/left/pallas_call | solution.py:39
  64.0 0.1 collective-permute-start
  64.1 1.5 %collective-permute-done.other = f32[512,128]{1,0:T(8,128)S(1)} collective-permute-done((f32[512,128]{1,0:T(8,128)S(1)}, f32[512,128]{1,0:T(8,128)S(1)}, u32[]{:S(2)}, u32[]{:S(2)}) %collective-permute-start) | collective-permute-done | bytes 262176 | tf_op jit(solution)/shard_map/ppermute | solution.py:260
  65.6 0.0 copy-done.3
  65.6 0.0 copy-done.4
  65.6 1.5 %gain.1 = f32[64,2,128]{2,1,0:T(2,128)} custom-call(s32[4,16]{1,0:T(4,128)S(1)} %bitcast.13, s32[4,16]{1,0:T(4,128)S(1)} %bitcast.14, f32[512,128]{1,0:T(8,128)S(1)} %get-tuple-element.15.own, f32[512,128]{1,0:T(8,128)S(1)} %collective-permute-done.other), custom_call_target="tpu_custom_call" | custom-call | tf_op jit(solution)/shard_map/gain/pallas_call | solution.py:39
  67.2 0.1 copy.10
  67.3 0.1 copy.12
  67.3 5.5 %all-to-all-start.2 = ((f32[64,2,128]{2,1,0:T(2,128)}), f32[64,2,128]{2,1,0:T(2,128)S(1)}, u32[]{:S(2)}, u32[]{:S(2)}) async-start(f32[64,2,128]{2,1,0:T(2,128)} %gain.1), calls=%async_computation.2 | async-start | bytes 131072 | tf_op jit(solution)/shard_map/all_to_all | solution.py:269
  72.8 0.0 copy-done
  72.8 0.0 copy-done.1
  72.8 0.3 route.1
  73.1 11.1 %all-to-all-done.2.gathered = f32[64,2,128]{2,1,0:T(2,128)S(1)} async-done(((f32[64,2,128]{2,1,0:T(2,128)}), f32[64,2,128]{2,1,0:T(2,128)S(1)}, u32[]{:S(2)}, u32[]{:S(2)}) %all-to-all-start.2) | async-done | bytes 65568 | tf_op jit(solution)/shard_map/all_to_all | solution.py:269
  84.2 0.0 copy-done.2
  84.2 0.9 %finish.1 = (f32[4,16]{1,0:T(4,128)}, f32[16,256]{1,0:T(8,128)}) custom-call(f32[64,2,128]{2,1,0:T(2,128)S(1)} %all-to-all-done.2.gathered, f32[16,256]{1,0:T(8,128)S(1)} %bitcast.12, s32[16,256]{1,0:T(8,128)S(1)} %route.1), custom_call_target="tpu_custom_call" | custom-call | tf_op jit(solution)/shard_map/finish/pallas_call | solution.py:39
  (1 shorter events, 0.0 us)
Async XLA Ops:
  57.8 7.8 %copy-start.3 = (s32[16,4]{0,1:T(4,128)S(1)}, s32[16,4]{0,1:T(4,128)}, u32[]{:S(2)}) copy-start(s32[16,4]{0,1:T(4,128)} %param.10) | copy-start | bytes 772
  57.8 7.8 %copy-start.4 = (s32[16,4]{0,1:T(4,128)S(1)}, s32[16,4]{0,1:T(4,128)}, u32[]{:S(2)}) copy-start(s32[16,4]{0,1:T(4,128)} %param.11) | copy-start | bytes 772
  57.8 15.0 %copy-start = (s32[256,256]{1,0:T(8,128)S(1)}, s32[256,256]{1,0:T(8,128)}, u32[]{:S(2)}) copy-start(s32[256,256]{1,0:T(8,128)} %bins.3) | copy-start | bytes 786436
  57.8 15.0 %copy-start.1 = (s32[256,16]{0,1:T(8,128)S(1)}, s32[256,16]{0,1:T(8,128)}, u32[]{:S(2)}) copy-start(s32[256,16]{0,1:T(8,128)} %param.8) | copy-start | bytes 49156
  57.8 26.4 %copy-start.2 = (f32[256,16]{0,1:T(8,128)S(1)}, f32[256,16]{0,1:T(8,128)}, u32[]{:S(2)}) copy-start(f32[256,16]{0,1:T(8,128)} %param.6) | copy-start | bytes 49156
  64.0 1.6 %collective-permute-start = (f32[512,128]{1,0:T(8,128)S(1)}, f32[512,128]{1,0:T(8,128)S(1)}, u32[]{:S(2)}, u32[]{:S(2)}) collective-permute-start(f32[512,128]{1,0:T(8,128)S(1)} %get-tuple-element.16), channel_id=1, source_target_pairs={{0,64},{64,0},{1,65},{65,1},{2,66},{66,2},{3,67},{67,3},{4,68},{68... | collective-permute-start | bytes 786440 | tf_op jit(solution)/shard_map/ppermute | solution.py:260
  67.3 16.9 %all-to-all-start.2 = ((f32[64,2,128]{2,1,0:T(2,128)}), f32[64,2,128]{2,1,0:T(2,128)S(1)}, u32[]{:S(2)}, u32[]{:S(2)}) async-start(f32[64,2,128]{2,1,0:T(2,128)} %gain.1), calls=%async_computation.2 | async-start | bytes 131072 | tf_op jit(solution)/shard_map/all_to_all | solution.py:269

commit v4 on v3

--- a/solution.py
+++ b/solution.py
@@ -47,14 +47,19 @@
     )(*args)
 
 
-def join_kernel(scores, nodes, labels, bins, joined, turned, label, node_buffer, label_buffer, columns, sems):
-    core = lax.axis_index("core")
+def join_kernel(
+    scores, nodes, labels, bins, pick_feature, pick_bin, joined, turned, label, target,
+    node_buffer, label_buffer, columns, picked, sems,
+):
+    core, quarter = lax.axis_index("core"), lax.axis_index("xh")
     start = pl.multiple_of(core * HALF, HALF)
     copies = [
         pltpu.make_async_copy(bins.at[pl.ds(start, HALF), :], columns, sems.at[0]),
         pltpu.make_async_copy(scores, joined.at[pl.ds(0, SHARD), :], sems.at[1]),
         pltpu.make_async_copy(nodes, node_buffer, sems.at[2]),
         pltpu.make_async_copy(labels, label_buffer, sems.at[3]),
+        pltpu.make_async_copy(pick_feature, picked.at[0], sems.at[4]),
+        pltpu.make_async_copy(pick_bin, picked.at[1], sems.at[5]),
     ]
     for copy in copies:
         copy.start()
@@ -64,6 +69,13 @@
     turned[...] = columns[...].astype(F32).T
     row = label_buffer[...].astype(F32)
     label[...] = jnp.broadcast_to(jnp.where(core == 0, row[:, :HALF], row[:, HALF:]), label.shape)
+    lane = lax.broadcasted_iota(jnp.int32, target.shape, 1) % (NODES * PART)
+    chosen = jnp.zeros(target.shape, jnp.int32)
+    for n in range(NODES):
+        for k in range(PART):
+            where = quarter * PART + k
+            chosen = jnp.where(lane == n * PART + k, picked[0, n, where] * BINS + picked[1, n, where], chosen)
+    target[...] = chosen
 
 
 def prepare_kernel(every, turned, label, send):
@@ -168,16 +180,10 @@
         away[row : row + BINS] = jnp.where(core == 0, second, first)
 
 
-def gain_kernel(pick_feature, pick_bin, own, other, spread):
-    quarter = lax.axis_index("xh")
+def gain_kernel(target, own, other, spread):
     group = lax.axis_index("z") * COLUMNS + lax.axis_index("y")
     lane = lax.broadcasted_iota(jnp.int32, (1, 128), 1)
-    target = jnp.zeros((1, 128), jnp.int32)
-    for n in range(NODES):
-        for k in range(PART):
-            chosen = pick_feature[n, quarter * PART + k] * BINS + pick_bin[n, quarter * PART + k]
-            target = jnp.where(lane % 32 == n * PART + k, chosen, target)
-    pick = target - group * (FEATS * BINS) - jnp.where(lane >= 64, FEATS * BINS // 2, 0)
+    pick = target[:1] - group * (FEATS * BINS) - jnp.where(lane >= 64, FEATS * BINS // 2, 0)
     line = lax.broadcasted_iota(jnp.int32, (BINS, 128), 0)
     best = jnp.full((BINS, 128), -jnp.inf, F32)
     sums = jnp.zeros((BINS, 128), F32)
@@ -236,14 +242,20 @@
     scores_t, nodes_t = scores.T, nodes.T
     shape = lambda *s: jax.ShapeDtypeStruct(s, F32)
 
-    inputs = [PIN(x) for x in (scores_t, nodes_t, labels[None], bins)]
-    joined, turned, label = call(
-        join_kernel, "join", (shape(2 * SHARD, rows), shape(bins.shape[1], HALF), shape(8, HALF)), [HBM] * 4, inputs,
+    inputs = [PIN(x) for x in (scores_t, nodes_t, labels[None], bins, pick_feature.T, pick_bin.T)]
+    joined, turned, label, target = call(
+        join_kernel, "join",
+        (
+            shape(2 * SHARD, rows), shape(bins.shape[1], HALF), shape(8, HALF),
+            jax.ShapeDtypeStruct((8, 128), jnp.int32),
+        ),
+        [HBM] * 6, inputs,
         scratch=[
             pltpu.VMEM((SHARD, rows), jnp.int32),
             pltpu.VMEM((1, rows), jnp.int32),
             pltpu.VMEM((HALF, bins.shape[1]), jnp.int32),
-            pltpu.SemaphoreType.DMA((4,)),
+            pltpu.SMEM((2, NODES, SHARD), jnp.int32),
+            pltpu.SemaphoreType.DMA((6,)),
         ],
     )
     every = lax.all_gather(joined, CLS)
@@ -258,14 +270,13 @@
         scratch=[pltpu.VMEM((FEATS * BINS, 128), F32)] + buffer + buffer, mib=32,
     )
     other = lax.ppermute(away, "core", [(0, 1), (1, 0)])
-    spread = call(
-        gain_kernel, "gain", shape(chips, 2, 128), [SMEM, SMEM, VMEM, VMEM], (pick_feature.T, pick_bin.T, own, other)
-    )
-    pick_feature, pick_bin, spread = lax.optimization_barrier((pick_feature, pick_bin, spread))
+    pick_feature, pick_bin, own = lax.optimization_barrier((pick_feature, pick_bin, own))
     picks = pick_feature * BINS + pick_bin
     route = call(
         route_kernel, "route", jax.ShapeDtypeStruct((SHARD, rows), jnp.int32), [VMEM] * 3, (picks, nodes_t, bins)
     )
+    other, route = lax.optimization_barrier((other, route))
+    spread = call(gain_kernel, "gain", shape(chips, 2, 128), [VMEM] * 3, (target, own, other))
     gathered = lax.all_to_all(spread, ROW, 0, 0)
     best, new_scores = call(
         finish_kernel, "finish", (shape(NODES, SHARD), shape(SHARD, rows)), [VMEM] * 3, (gathered, scores_t, route)

time: 86.3 us -> 84.1 us (0.975)
  blocking collectives: 56 us -> 72.1 us
  waiting for transfers between devices: 12.6 us -> 1.05 us
  starting transfers between devices: 5.56 us -> 0.09 us
  Pallas kernels: 10.1 us -> 8.84 us
    all_to_all x0 -> x1, blocking collectives: none -> 16.1 us  [per_device(): gathered = lax.all_to_all(spread, ROW, 0, 0)]
    all_to_all x1 -> x0, waiting for transfers between devices: 11.1 us -> none  [per_device(): gathered = lax.all_to_all(spread, ROW, 0, 0)]
    all_to_all x1 -> x0, starting transfers between devices: 5.47 us -> none  [per_device(): gathered = lax.all_to_all(spread, ROW, 0, 0)]
    pallas_call x7, Pallas kernels: 10.1 us -> 8.84 us  [call(): pl.pallas_call(kernel, out_shape=shapes, in_specs=specs, out_specs=(VMEM,...]
  transfers between devices with their start and end apart: 2 -> 1, of which waited for: 2 -> 1; matrix products, arithmetic and copies ran while one was open for 0% -> 0% of each run, Pallas kernels for 0% -> 0%
where the time goes in v4:
time: 84.1 us; the launch traced here: 82.9 us
  blocking collectives  72.1 us (86%)
  Pallas kernels  8.84 us (11%)
  waiting for transfers between devices  1.05 us (1%)
    all_to_all x1, blocking collectives, per_device(): taken = lax.all_to_all(send, ('xh', 'y'), 0, 0)  26.4 us
    all_to_all x1, blocking collectives, per_device(): came = lax.all_to_all(send, 'z', 0, 0)  24.2 us
    all_to_all x1, blocking collectives, per_device(): gathered = lax.all_to_all(spread, ROW, 0, 0)  16.1 us
    pallas_call x7, Pallas kernels, call(): pl.pallas_call(kernel, out_shape=shapes, in_specs=specs, out_specs=(VMEM,...  8.84 us
    all_gather x1, blocking collectives, per_device(): every = lax.all_gather(joined, CLS)  5.43 us
  transfers between devices with their start and end apart: 1, of which 1 were waited for; matrix products, arithmetic and copies ran while one was open for 0% of the time, Pallas kernels for 0%

profile of v4, /device:TPU:8, one launch (start us, length us, event | category | flops | bytes accessed | tf_op | source)
XLA Modules:
  0.0 82.9 jit_solution(8708157331233388350)
XLA Ops:
  0.6 1.1 %join.1 = (f32[32,256]{1,0:T(8,128)S(1)}, f32[256,128]{1,0:T(8,128)S(1)}, f32[8,128]{1,0:T(8,128)S(1)}, s32[8,128]{1,0:T(8,128)S(1)}) custom-call(f32[16,256]{1,0:T(8,128)} %bitcast.11, s32[16,256]{1,0:T(8,128)} %bitcast.9, s32[1,256]{1,0:T(1,128)} %bitcast.15, s32[256,256]{1,0:T(8,128)} %bins.3, s32[4,16]{1,0:T(4,128)} %bitcast.13, s32[4,16]{1,0:T(4,128)} %bitcast.14), custom_call_target="tpu_custom_call" | custom-call | tf_op jit(solution)/shard_map/join/pallas_call | solution.py:39
  1.7 5.4 %all-gather = f32[128,256]{1,0:T(8,128)S(1)} all-gather(f32[32,256]{1,0:T(8,128)S(1)} %get-tuple-element.16), channel_id=2, replica_groups=mesh['xl'=2,'core'=2,'xh'=2,'z'=8,'y'=4] {'xl','core'}, dimensions={0}, use_global_device_ids=true | all-gather | bytes 163840 | tf_op jit(solution)/shard_map/all_gather | solution.py:261
  7.2 0.1 prepare.1
  7.2 24.2 %all_to_all.15.came = f32[8,104,128]{2,1,0:T(8,128)S(1)} all-to-all(f32[8,104,128]{2,1,0:T(8,128)S(1)} %prepare.1), channel_id=1, replica_groups=mesh['xl'=2,'core'=2,'xh'=2,'z'=8,'y'=4] {'z'}, dimensions={0} | all-to-all | bytes 851968 | tf_op jit(solution)/shard_map/all_to_all | solution.py:263
  31.4 0.1 relay.1
  31.5 26.4 %all_to_all.16.taken = f32[8,328,128]{2,1,0:T(8,128)S(1)} all-to-all(f32[8,328,128]{2,1,0:T(8,128)S(1)} %relay.1), channel_id=1, replica_groups=mesh['xl'=2,'core'=2,'xh'=2,'z'=8,'y'=4] {'xh','y'}, dimensions={0} | all-to-all | bytes 2686976 | tf_op jit(solution)/shard_map/all_to_all | solution.py:265
  57.9 0.0 copy-start.3
  57.9 0.0 copy-start.4
  57.9 0.0 copy-start
  57.9 0.0 copy-start.1
  57.9 0.0 copy-start.2
  57.9 6.2 %left.1 = (f32[512,128]{1,0:T(8,128)S(1)}, f32[512,128]{1,0:T(8,128)S(1)}) custom-call(f32[8,328,128]{2,1,0:T(8,128)S(1)} %all_to_all.16.taken), custom_call_target="tpu_custom_call" | custom-call | tf_op jit(solution)/shard_map/left/pallas_call | solution.py:39
  64.0 0.1 collective-permute-start
  64.2 0.0 copy-done.3
  64.2 0.1 copy.10
  64.2 0.0 copy-done.4
  64.2 0.1 copy.12
  64.3 0.0 copy-done
  64.3 0.0 copy-done.1
  64.3 0.3 route.1
  64.6 1.1 %collective-permute-done.other = f32[512,128]{1,0:T(8,128)S(1)} collective-permute-done((f32[512,128]{1,0:T(8,128)S(1)}, f32[512,128]{1,0:T(8,128)S(1)}, u32[]{:S(2)}, u32[]{:S(2)}) %collective-permute-start) | collective-permute-done | bytes 262176 | tf_op jit(solution)/shard_map/ppermute | solution.py:272
  65.7 0.3 gain.1
  66.0 16.1 %all_to_all.17.gathered = f32[64,2,128]{2,1,0:T(2,128)S(1)} all-to-all(f32[64,2,128]{2,1,0:T(2,128)S(1)} %gain.1), channel_id=1, replica_groups=mesh['xl'=2,'core'=2,'xh'=2,'z'=8,'y'=4] {'xh','z','y'}, dimensions={0} | all-to-all | bytes 131072 | tf_op jit(solution)/shard_map/all_to_all | solution.py:280
  82.0 0.0 copy-done.2
  82.0 0.9 %finish.1 = (f32[4,16]{1,0:T(4,128)}, f32[16,256]{1,0:T(8,128)}) custom-call(f32[64,2,128]{2,1,0:T(2,128)S(1)} %all_to_all.17.gathered, f32[16,256]{1,0:T(8,128)S(1)} %bitcast.12, s32[16,256]{1,0:T(8,128)S(1)} %route.1), custom_call_target="tpu_custom_call" | custom-call | tf_op jit(solution)/shard_map/finish/pallas_call | solution.py:39
  (1 shorter events, 0.0 us)
Async XLA Ops:
  57.9 6.3 %copy-start.3 = (s32[16,4]{0,1:T(4,128)S(1)}, s32[16,4]{0,1:T(4,128)}, u32[]{:S(2)}) copy-start(s32[16,4]{0,1:T(4,128)} %param.10) | copy-start | bytes 772
  57.9 6.4 %copy-start.4 = (s32[16,4]{0,1:T(4,128)S(1)}, s32[16,4]{0,1:T(4,128)}, u32[]{:S(2)}) copy-start(s32[16,4]{0,1:T(4,128)} %param.11) | copy-start | bytes 772
  57.9 6.5 %copy-start = (s32[256,256]{1,0:T(8,128)S(1)}, s32[256,256]{1,0:T(8,128)}, u32[]{:S(2)}) copy-start(s32[256,256]{1,0:T(8,128)} %bins.3) | copy-start | bytes 786436
  57.9 6.5 %copy-start.1 = (s32[256,16]{0,1:T(8,128)S(1)}, s32[256,16]{0,1:T(8,128)}, u32[]{:S(2)}) copy-start(s32[256,16]{0,1:T(8,128)} %param.8) | copy-start | bytes 49156
  57.9 24.2 %copy-start.2 = (f32[256,16]{0,1:T(8,128)S(1)}, f32[256,16]{0,1:T(8,128)}, u32[]{:S(2)}) copy-start(f32[256,16]{0,1:T(8,128)} %param.6) | copy-start | bytes 49156
  64.0 1.6 %collective-permute-start = (f32[512,128]{1,0:T(8,128)S(1)}, f32[512,128]{1,0:T(8,128)S(1)}, u32[]{:S(2)}, u32[]{:S(2)}) collective-permute-start(f32[512,128]{1,0:T(8,128)S(1)} %get-tuple-element.21), channel_id=1, source_target_pairs={{0,64},{64,0},{1,65},{65,1},{2,66},{66,2},{3,67},{67,3},{4,68},{68... | collective-permute-start | bytes 786440 | tf_op jit(solution)/shard_map/ppermute | solution.py:272

commit v5 on v4

--- a/solution.py
+++ b/solution.py
@@ -79,39 +79,40 @@
 
 
 def prepare_kernel(every, turned, label, send):
-    xl, core = lax.axis_index("xl"), lax.axis_index("core")
+    xl, core, xh = (lax.axis_index(a) for a in ("xl", "core", "xh"))
 
     def half(x):
         return jnp.where(core == 0, x[..., :HALF], x[..., HALF:])
 
     scores = [half(every[i, :SHARD, :]) for i in range(4)]
-    nodes = [half(every[i, SHARD:, :]) for i in range(4)]
     top = jnp.max(jnp.maximum(jnp.maximum(scores[0], scores[1]), jnp.maximum(scores[2], scores[3])), axis=0, keepdims=True)
     exponent = [jnp.exp(s - top) for s in scores]
     denominator = jnp.sum((exponent[0] + exponent[1]) + (exponent[2] + exponent[3]), axis=0, keepdims=True)
-    prob = [jnp.where(xl == 0, exponent[i], exponent[2 + i]) / denominator for i in range(2)]
-    node = [jnp.where(xl == 0, nodes[i], nodes[2 + i]) for i in range(2)]
+    parts = []
+    for q in range(2):
+        low = (xl == 0) == (xh == q)
+        part = slice(q * PART, (q + 1) * PART)
+        for shard in range(2):
+            parts.append(jnp.where(low, exponent[shard][part], exponent[2 + shard][part]) / denominator)
+        part = slice(SHARD + q * PART, SHARD + (q + 1) * PART)
+        for shard in range(2):
+            parts.append(half(jnp.where(low, every[shard, part, :], every[2 + shard, part, :])))
     width = COLUMNS * FEATS
     for layer in range(LAYERS):
-        for i, part in enumerate(prob + node):
-            send[layer, i * SHARD : (i + 1) * SHARD] = part
+        for i, part in enumerate(parts):
+            send[layer, i * PART : (i + 1) * PART] = part
         send[layer, 64:96] = turned[layer * width : (layer + 1) * width]
         send[layer, 96:104] = label[...]
 
 
 def relay_kernel(came, send):
     for layer in range(LAYERS):
+        row = layer * BLOCK
         for q in range(2):
-            parts = [came[layer, i * SHARD + q * PART : i * SHARD + (q + 1) * PART] for i in range(4)]
             for y in range(COLUMNS):
-                for i in range(4):
-                    row = layer * BLOCK + i * PART
-                    send[q * COLUMNS + y, row : row + PART] = parts[i]
-        for y in range(COLUMNS):
-            columns = came[layer, 64 + y * FEATS : 64 + (y + 1) * FEATS]
-            for q in range(2):
-                row = layer * BLOCK + 4 * PART
-                send[q * COLUMNS + y, row : row + FEATS] = columns
+                peer = q * COLUMNS + y
+                send[peer, row : row + 4 * PART] = came[layer, q * 4 * PART : (q + 1) * 4 * PART]
+                send[peer, row + 4 * PART : row + BLOCK] = came[layer, 64 + y * FEATS : 64 + (y + 1) * FEATS]
     labels = jnp.concatenate([came[layer, 96:97] for layer in range(LAYERS)], axis=0)
     for peer in range(PEERS):
         send[peer, LAYERS * BLOCK :] = labels
@@ -236,6 +237,13 @@
         new_scores[part] = scores[part] + learn_rate * leaf
 
 
+def neighbours():
+    return [
+        [((first if xh == 0 else 1 - first) * 2 + xh) * COLUMNS + y for xh in range(2) for y in range(COLUMNS)]
+        for first in range(2)
+    ]
+
+
 def per_device(scores, labels, nodes, bins, pick_feature, pick_bin):
     rows = 2 * HALF
     chips = PEERS * LAYERS
@@ -262,7 +270,7 @@
     send = call(prepare_kernel, "prepare", shape(LAYERS, 104, HALF), [VMEM] * 3, (every, turned, label))
     came = lax.all_to_all(send, "z", 0, 0)
     send = call(relay_kernel, "relay", shape(PEERS, LAYERS * (BLOCK + 1), HALF), [VMEM], (came,))
-    taken = lax.all_to_all(send, ("xh", "y"), 0, 0)
+    taken = lax.all_to_all(send, ("xl", "xh", "y"), 0, 0, axis_index_groups=neighbours())
     buffer = [pltpu.VMEM((128, LAYERS * HALF), BF16), pltpu.VMEM((FEATS * BINS, LAYERS * HALF), BF16)]
     half = shape(FEATS * BINS // 2, 128)
     own, away = call(

time: 84.1 us -> 83.6 us (level)
  no operation moved by 1% of the time
where the time goes in v5:
time: 83.6 us; the launch traced here: 82.4 us
  blocking collectives  71.5 us (86%)
  Pallas kernels  8.84 us (11%)
  waiting for transfers between devices  1.05 us (1%)
    all_to_all x1, blocking collectives, per_device(): lax.all_to_all(send, ('xl', 'xh', 'y'), 0, 0, axis_index_groups=neighbour...  25.8 us
    all_to_all x1, blocking collectives, per_device(): came = lax.all_to_all(send, 'z', 0, 0)  24.2 us
    all_to_all x1, blocking collectives, per_device(): gathered = lax.all_to_all(spread, ROW, 0, 0)  16.1 us
    pallas_call x7, Pallas kernels, call(): pl.pallas_call(kernel, out_shape=shapes, in_specs=specs, out_specs=(VMEM,...  8.84 us
    all_gather x1, blocking collectives, per_device(): every = lax.all_gather(joined, CLS)  5.43 us
  transfers between devices with their start and end apart: 1, of which 1 were waited for; matrix products, arithmetic and copies ran while one was open for 0% of the time, Pallas kernels for 0%

profile of v5, /device:TPU:8, one launch (start us, length us, event | category | flops | bytes accessed | tf_op | source)
XLA Modules:
  0.0 82.4 jit_solution(8467614265471223586)
XLA Ops:
  0.6 1.1 %join.1 = (f32[32,256]{1,0:T(8,128)S(1)}, f32[256,128]{1,0:T(8,128)S(1)}, f32[8,128]{1,0:T(8,128)S(1)}, s32[8,128]{1,0:T(8,128)S(1)}) custom-call(f32[16,256]{1,0:T(8,128)} %bitcast.11, s32[16,256]{1,0:T(8,128)} %bitcast.9, s32[1,256]{1,0:T(1,128)} %bitcast.15, s32[256,256]{1,0:T(8,128)} %bins.3, s32[4,16]{1,0:T(4,128)} %bitcast.13, s32[4,16]{1,0:T(4,128)} %bitcast.14), custom_call_target="tpu_custom_call" | custom-call | tf_op jit(solution)/shard_map/join/pallas_call | solution.py:39
  1.7 5.4 %all-gather = f32[128,256]{1,0:T(8,128)S(1)} all-gather(f32[32,256]{1,0:T(8,128)S(1)} %get-tuple-element.16), channel_id=2, replica_groups=mesh['xl'=2,'core'=2,'xh'=2,'z'=8,'y'=4] {'xl','core'}, dimensions={0}, use_global_device_ids=true | all-gather | bytes 163840 | tf_op jit(solution)/shard_map/all_gather | solution.py:269
  7.2 0.1 prepare.1
  7.2 24.2 %all_to_all.15.came = f32[8,104,128]{2,1,0:T(8,128)S(1)} all-to-all(f32[8,104,128]{2,1,0:T(8,128)S(1)} %prepare.1), channel_id=1, replica_groups=mesh['xl'=2,'core'=2,'xh'=2,'z'=8,'y'=4] {'z'}, dimensions={0} | all-to-all | bytes 851968 | tf_op jit(solution)/shard_map/all_to_all | solution.py:271
  31.4 0.1 relay.1
  31.5 25.8 %all_to_all.16.taken = f32[8,328,128]{2,1,0:T(8,128)S(1)} all-to-all(f32[8,328,128]{2,1,0:T(8,128)S(1)} %relay.1), channel_id=1, replica_groups={{0,1,2,3,160,161,162,163},{128,129,130,131,32,33,34,35},{4,5,6,7,164,16..., dimensions={0} | all-to-all | bytes 2686976 | tf_op jit(solution)/shard_map/all_to_all | solution.py:273
  57.3 0.0 copy-start.3
  57.3 0.0 copy-start.4
  57.3 0.0 copy-start
  57.3 0.0 copy-start.1
  57.3 0.0 copy-start.2
  57.3 6.2 %left.1 = (f32[512,128]{1,0:T(8,128)S(1)}, f32[512,128]{1,0:T(8,128)S(1)}) custom-call(f32[8,328,128]{2,1,0:T(8,128)S(1)} %all_to_all.16.taken), custom_call_target="tpu_custom_call" | custom-call | tf_op jit(solution)/shard_map/left/pallas_call | solution.py:39
  63.5 0.1 collective-permute-start
  63.6 0.0 copy-done.3
  63.6 0.1 copy.10
  63.7 0.0 copy-done.4
  63.7 0.1 copy.12
  63.8 0.0 copy-done
  63.8 0.0 copy-done.1
  63.8 0.3 route.1
  64.1 1.1 %collective-permute-done.other = f32[512,128]{1,0:T(8,128)S(1)} collective-permute-done((f32[512,128]{1,0:T(8,128)S(1)}, f32[512,128]{1,0:T(8,128)S(1)}, u32[]{:S(2)}, u32[]{:S(2)}) %collective-permute-start) | collective-permute-done | bytes 262176 | tf_op jit(solution)/shard_map/ppermute | solution.py:280
  65.1 0.3 gain.1
  65.4 16.1 %all_to_all.17.gathered = f32[64,2,128]{2,1,0:T(2,128)S(1)} all-to-all(f32[64,2,128]{2,1,0:T(2,128)S(1)} %gain.1), channel_id=1, replica_groups=mesh['xl'=2,'core'=2,'xh'=2,'z'=8,'y'=4] {'xh','z','y'}, dimensions={0} | all-to-all | bytes 131072 | tf_op jit(solution)/shard_map/all_to_all | solution.py:288
  81.5 0.0 copy-done.2
  81.5 0.9 %finish.1 = (f32[4,16]{1,0:T(4,128)}, f32[16,256]{1,0:T(8,128)}) custom-call(f32[64,2,128]{2,1,0:T(2,128)S(1)} %all_to_all.17.gathered, f32[16,256]{1,0:T(8,128)S(1)} %bitcast.12, s32[16,256]{1,0:T(8,128)S(1)} %route.1), custom_call_target="tpu_custom_call" | custom-call | tf_op jit(solution)/shard_map/finish/pallas_call | solution.py:39
  (1 shorter events, 0.0 us)
Async XLA Ops:
  57.3 6.3 %copy-start.3 = (s32[16,4]{0,1:T(4,128)S(1)}, s32[16,4]{0,1:T(4,128)}, u32[]{:S(2)}) copy-start(s32[16,4]{0,1:T(4,128)} %param.10) | copy-start | bytes 772
  57.3 6.4 %copy-start.4 = (s32[16,4]{0,1:T(4,128)S(1)}, s32[16,4]{0,1:T(4,128)}, u32[]{:S(2)}) copy-start(s32[16,4]{0,1:T(4,128)} %param.11) | copy-start | bytes 772
  57.3 6.5 %copy-start = (s32[256,256]{1,0:T(8,128)S(1)}, s32[256,256]{1,0:T(8,128)}, u32[]{:S(2)}) copy-start(s32[256,256]{1,0:T(8,128)} %bins.3) | copy-start | bytes 786436
  57.3 6.5 %copy-start.1 = (s32[256,16]{0,1:T(8,128)S(1)}, s32[256,16]{0,1:T(8,128)}, u32[]{:S(2)}) copy-start(s32[256,16]{0,1:T(8,128)} %param.8) | copy-start | bytes 49156
  57.3 24.2 %copy-start.2 = (f32[256,16]{0,1:T(8,128)S(1)}, f32[256,16]{0,1:T(8,128)}, u32[]{:S(2)}) copy-start(f32[256,16]{0,1:T(8,128)} %param.6) | copy-start | bytes 49156
  63.5 1.6 %collective-permute-start = (f32[512,128]{1,0:T(8,128)S(1)}, f32[512,128]{1,0:T(8,128)S(1)}, u32[]{:S(2)}, u32[]{:S(2)}) collective-permute-start(f32[512,128]{1,0:T(8,128)S(1)} %get-tuple-element.21), channel_id=1, source_target_pairs={{0,64},{64,0},{1,65},{65,1},{2,66},{66,2},{3,67},{67,3},{4,68},{68... | collective-permute-start | bytes 786440 | tf_op jit(solution)/shard_map/ppermute | solution.py:280

commit v6 on v5

--- a/solution.py
+++ b/solution.py
@@ -132,14 +132,17 @@
     route[...] = out
 
 
-def left_kernel(taken, own, away, left, *buffers):
+TURNED = 6
+
+
+def left_kernel(taken, own, away, left, wide, *buffers):
     xl, core, quarter = (lax.axis_index(a) for a in ("xl", "core", "xh"))
     class_id = lax.broadcasted_iota(jnp.int32, (PART, HALF), 0) + quarter * PART
     ids = [(class_id + (2 * xl + shard) * SHARD).astype(F32) for shard in range(2)]
     bin_range = lax.broadcasted_iota(jnp.int32, (BINS, HALF), 0).astype(BF16)
     one, zero = jnp.ones((), BF16), jnp.zeros((), BF16)
 
-    def build(source, paired, mask):
+    def build(source, paired, mask, turned):
         for layer in range(LAYERS):
             lanes = slice(layer * HALF, (layer + 1) * HALF)
             base = layer * BLOCK
@@ -152,16 +155,22 @@
                 for value in (prob - target, 2.0 * prob * (1.0 - prob)):
                     tiles += [jnp.where(node == float(n), value, 0.0) for n in range(NODES)]
             paired[:, lanes] = jnp.concatenate(tiles, axis=0).astype(BF16)
+            masks = []
             for f in range(FEATS):
                 row = taken[source, base + 4 * PART + f : base + 4 * PART + f + 1]
                 row = jnp.broadcast_to(row, (BINS, HALF)).astype(BF16)
-                mask[f * BINS : (f + 1) * BINS, lanes] = jnp.where(bin_range >= row, one, zero)
-
-    def multiply(paired, mask):
-        left[...] += lax.dot_general(mask[...], paired[...], LAST_DIMS, preferred_element_type=F32)
-
-    even, odd = buffers[:2], buffers[2:]
+                masks.append(jnp.where(bin_range >= row, one, zero))
+            turned[lanes, :] = jnp.concatenate(masks[:TURNED], axis=0).T
+            for i, tile in enumerate(masks[TURNED:]):
+                mask[i * BINS : (i + 1) * BINS, lanes] = tile
+
+    def multiply(paired, mask, turned):
+        wide[...] += jnp.dot(paired[...], turned[...], preferred_element_type=F32)
+        left[TURNED * BINS :] += lax.dot_general(mask[...], paired[...], LAST_DIMS, preferred_element_type=F32)
+
+    even, odd = buffers[:3], buffers[3:]
     left[...] = jnp.zeros_like(left)
+    wide[...] = jnp.zeros_like(wide)
     build(0, *even)
 
     @pl.loop(0, PEERS // 2)
@@ -171,6 +180,8 @@
         build(jnp.minimum(2 * pair + 2, PEERS - 1), *even)
         multiply(*odd)
 
+    for f in range(TURNED):
+        left[f * BINS : (f + 1) * BINS] = wide[:, f * BINS : (f + 1) * BINS].T
     middle = FEATS * BINS // 2
     low = lax.broadcasted_iota(jnp.int32, (BINS, 128), 1) < 64
     for row in range(0, middle, BINS):
@@ -271,11 +282,16 @@
     came = lax.all_to_all(send, "z", 0, 0)
     send = call(relay_kernel, "relay", shape(PEERS, LAYERS * (BLOCK + 1), HALF), [VMEM], (came,))
     taken = lax.all_to_all(send, ("xl", "xh", "y"), 0, 0, axis_index_groups=neighbours())
-    buffer = [pltpu.VMEM((128, LAYERS * HALF), BF16), pltpu.VMEM((FEATS * BINS, LAYERS * HALF), BF16)]
+    depth = LAYERS * HALF
+    buffer = [
+        pltpu.VMEM((128, depth), BF16),
+        pltpu.VMEM(((FEATS - TURNED) * BINS, depth), BF16),
+        pltpu.VMEM((depth, TURNED * BINS), BF16),
+    ]
     half = shape(FEATS * BINS // 2, 128)
     own, away = call(
         left_kernel, "left", (half, half), [VMEM], (taken,),
-        scratch=[pltpu.VMEM((FEATS * BINS, 128), F32)] + buffer + buffer, mib=32,
+        scratch=[pltpu.VMEM((FEATS * BINS, 128), F32), pltpu.VMEM((128, TURNED * BINS), F32)] + buffer + buffer, mib=32,
     )
     other = lax.ppermute(away, "core", [(0, 1), (1, 0)])
     pick_feature, pick_bin, own = lax.optimization_barrier((pick_feature, pick_bin, own))

time: 83.6 us -> 82.3 us (0.984)
  Pallas kernels: 8.84 us -> 7.61 us
    pallas_call x7, Pallas kernels: 8.84 us -> 7.61 us  [call(): pl.pallas_call(kernel, out_shape=shapes, in_specs=specs, out_specs=(VMEM,...]
where the time goes in v6:
time: 82.3 us; the launch traced here: 81.1 us
  blocking collectives  71.5 us (87%)
  Pallas kernels  7.61 us (9%)
  waiting for transfers between devices  1.05 us (1%)
    all_to_all x1, blocking collectives, per_device(): lax.all_to_all(send, ('xl', 'xh', 'y'), 0, 0, axis_index_groups=neighbour...  25.8 us
    all_to_all x1, blocking collectives, per_device(): came = lax.all_to_all(send, 'z', 0, 0)  24.2 us
    all_to_all x1, blocking collectives, per_device(): gathered = lax.all_to_all(spread, ROW, 0, 0)  16.1 us
    pallas_call x7, Pallas kernels, call(): pl.pallas_call(kernel, out_shape=shapes, in_specs=specs, out_specs=(VMEM,...  7.61 us
    all_gather x1, blocking collectives, per_device(): every = lax.all_gather(joined, CLS)  5.43 us
  transfers between devices with their start and end apart: 1, of which 1 were waited for; matrix products, arithmetic and copies ran while one was open for 0% of the time, Pallas kernels for 0%

profile of v6, /device:TPU:8, one launch (start us, length us, event | category | flops | bytes accessed | tf_op | source)
XLA Modules:
  0.0 81.1 jit_solution(2714023547819833345)
XLA Ops:
  0.6 1.1 %join.1 = (f32[32,256]{1,0:T(8,128)S(1)}, f32[256,128]{1,0:T(8,128)S(1)}, f32[8,128]{1,0:T(8,128)S(1)}, s32[8,128]{1,0:T(8,128)S(1)}) custom-call(f32[16,256]{1,0:T(8,128)} %bitcast.11, s32[16,256]{1,0:T(8,128)} %bitcast.9, s32[1,256]{1,0:T(1,128)} %bitcast.15, s32[256,256]{1,0:T(8,128)} %bins.3, s32[4,16]{1,0:T(4,128)} %bitcast.13, s32[4,16]{1,0:T(4,128)} %bitcast.14), custom_call_target="tpu_custom_call" | custom-call | tf_op jit(solution)/shard_map/join/pallas_call | solution.py:39
  1.7 5.4 %all-gather = f32[128,256]{1,0:T(8,128)S(1)} all-gather(f32[32,256]{1,0:T(8,128)S(1)} %get-tuple-element.16), channel_id=2, replica_groups=mesh['xl'=2,'core'=2,'xh'=2,'z'=8,'y'=4] {'xl','core'}, dimensions={0}, use_global_device_ids=true | all-gather | bytes 163840 | tf_op jit(solution)/shard_map/all_gather | solution.py:280
  7.2 0.1 prepare.1
  7.2 24.2 %all_to_all.15.came = f32[8,104,128]{2,1,0:T(8,128)S(1)} all-to-all(f32[8,104,128]{2,1,0:T(8,128)S(1)} %prepare.1), channel_id=1, replica_groups=mesh['xl'=2,'core'=2,'xh'=2,'z'=8,'y'=4] {'z'}, dimensions={0} | all-to-all | bytes 851968 | tf_op jit(solution)/shard_map/all_to_all | solution.py:282
  31.4 0.1 relay.1
  31.5 25.8 %all_to_all.16.taken = f32[8,328,128]{2,1,0:T(8,128)S(1)} all-to-all(f32[8,328,128]{2,1,0:T(8,128)S(1)} %relay.1), channel_id=1, replica_groups={{0,1,2,3,160,161,162,163},{128,129,130,131,32,33,34,35},{4,5,6,7,164,16..., dimensions={0} | all-to-all | bytes 2686976 | tf_op jit(solution)/shard_map/all_to_all | solution.py:284
  57.3 0.0 copy-start.3
  57.3 0.0 copy-start.4
  57.3 0.0 copy-start
  57.3 0.0 copy-start.1
  57.3 0.0 copy-start.2
  57.3 4.9 %left.1 = (f32[512,128]{1,0:T(8,128)S(1)}, f32[512,128]{1,0:T(8,128)S(1)}) custom-call(f32[8,328,128]{2,1,0:T(8,128)S(1)} %all_to_all.16.taken), custom_call_target="tpu_custom_call" | custom-call | tf_op jit(solution)/shard_map/left/pallas_call | solution.py:39
  62.3 0.1 collective-permute-start
  62.4 0.0 copy-done.3
  62.4 0.1 copy.10
  62.5 0.0 copy-done.4
  62.5 0.1 copy.12
  62.5 0.0 copy-done
  62.5 0.0 copy-done.1
  62.6 0.3 route.1
  62.8 1.1 %collective-permute-done.other = f32[512,128]{1,0:T(8,128)S(1)} collective-permute-done((f32[512,128]{1,0:T(8,128)S(1)}, f32[512,128]{1,0:T(8,128)S(1)}, u32[]{:S(2)}, u32[]{:S(2)}) %collective-permute-start) | collective-permute-done | bytes 262176 | tf_op jit(solution)/shard_map/ppermute | solution.py:296
  63.9 0.3 gain.1
  64.2 16.1 %all_to_all.17.gathered = f32[64,2,128]{2,1,0:T(2,128)S(1)} all-to-all(f32[64,2,128]{2,1,0:T(2,128)S(1)} %gain.1), channel_id=1, replica_groups=mesh['xl'=2,'core'=2,'xh'=2,'z'=8,'y'=4] {'xh','z','y'}, dimensions={0} | all-to-all | bytes 131072 | tf_op jit(solution)/shard_map/all_to_all | solution.py:304
  80.2 0.0 copy-done.2
  80.2 0.9 %finish.1 = (f32[4,16]{1,0:T(4,128)}, f32[16,256]{1,0:T(8,128)}) custom-call(f32[64,2,128]{2,1,0:T(2,128)S(1)} %all_to_all.17.gathered, f32[16,256]{1,0:T(8,128)S(1)} %bitcast.12, s32[16,256]{1,0:T(8,128)S(1)} %route.1), custom_call_target="tpu_custom_call" | custom-call | tf_op jit(solution)/shard_map/finish/pallas_call | solution.py:39
  (1 shorter events, 0.0 us)
Async XLA Ops:
  57.3 5.1 %copy-start.3 = (s32[16,4]{0,1:T(4,128)S(1)}, s32[16,4]{0,1:T(4,128)}, u32[]{:S(2)}) copy-start(s32[16,4]{0,1:T(4,128)} %param.10) | copy-start | bytes 772
  57.3 5.2 %copy-start.4 = (s32[16,4]{0,1:T(4,128)S(1)}, s32[16,4]{0,1:T(4,128)}, u32[]{:S(2)}) copy-start(s32[16,4]{0,1:T(4,128)} %param.11) | copy-start | bytes 772
  57.3 5.2 %copy-start = (s32[256,256]{1,0:T(8,128)S(1)}, s32[256,256]{1,0:T(8,128)}, u32[]{:S(2)}) copy-start(s32[256,256]{1,0:T(8,128)} %bins.3) | copy-start | bytes 786436
  57.3 5.2 %copy-start.1 = (s32[256,16]{0,1:T(8,128)S(1)}, s32[256,16]{0,1:T(8,128)}, u32[]{:S(2)}) copy-start(s32[256,16]{0,1:T(8,128)} %param.8) | copy-start | bytes 49156
  57.3 22.9 %copy-start.2 = (f32[256,16]{0,1:T(8,128)S(1)}, f32[256,16]{0,1:T(8,128)}, u32[]{:S(2)}) copy-start(f32[256,16]{0,1:T(8,128)} %param.6) | copy-start | bytes 49156
  62.3 1.6 %collective-permute-start = (f32[512,128]{1,0:T(8,128)S(1)}, f32[512,128]{1,0:T(8,128)S(1)}, u32[]{:S(2)}, u32[]{:S(2)}) collective-permute-start(f32[512,128]{1,0:T(8,128)S(1)} %get-tuple-element.21), channel_id=1, source_target_pairs={{0,64},{64,0},{1,65},{65,1},{2,66},{66,2},{3,67},{67,3},{4,68},{68... | collective-permute-start | bytes 786440 | tf_op jit(solution)/shard_map/ppermute | solution.py:296

commit v7 on v6

--- a/solution.py
+++ b/solution.py
@@ -132,7 +132,8 @@
     route[...] = out
 
 
-TURNED = 6
+TURNED = (0, 1, 2, 4, 5, 6)
+STREAMED = (3, 7)
 
 
 def left_kernel(taken, own, away, left, wide, *buffers):
@@ -160,36 +161,43 @@
                 row = taken[source, base + 4 * PART + f : base + 4 * PART + f + 1]
                 row = jnp.broadcast_to(row, (BINS, HALF)).astype(BF16)
                 masks.append(jnp.where(bin_range >= row, one, zero))
-            turned[lanes, :] = jnp.concatenate(masks[:TURNED], axis=0).T
-            for i, tile in enumerate(masks[TURNED:]):
-                mask[i * BINS : (i + 1) * BINS, lanes] = tile
+            turned[lanes, :] = jnp.concatenate([masks[f] for f in TURNED], axis=0).T
+            for i, f in enumerate(STREAMED):
+                mask[i * BINS : (i + 1) * BINS, lanes] = masks[f]
 
     def multiply(paired, mask, turned):
         wide[...] += jnp.dot(paired[...], turned[...], preferred_element_type=F32)
-        left[TURNED * BINS :] += lax.dot_general(mask[...], paired[...], LAST_DIMS, preferred_element_type=F32)
+        left[...] += lax.dot_general(mask[...], paired[...], LAST_DIMS, preferred_element_type=F32)
 
     even, odd = buffers[:3], buffers[3:]
     left[...] = jnp.zeros_like(left)
     wide[...] = jnp.zeros_like(wide)
     build(0, *even)
 
-    @pl.loop(0, PEERS // 2)
+    @pl.loop(0, PEERS // 2 - 1)
     def _(pair):
         build(2 * pair + 1, *odd)
         multiply(*even)
-        build(jnp.minimum(2 * pair + 2, PEERS - 1), *even)
+        build(2 * pair + 2, *even)
         multiply(*odd)
 
-    for f in range(TURNED):
-        left[f * BINS : (f + 1) * BINS] = wide[:, f * BINS : (f + 1) * BINS].T
-    middle = FEATS * BINS // 2
+    build(PEERS - 1, *odd)
+    multiply(*even)
+    multiply(*odd)
+
+    for out, shard in ((own, core), (away, 1 - core)):
+        rows = pl.ds(pl.multiple_of(shard * 64, 64), 64)
+        for i, f in enumerate(TURNED[: len(TURNED) // 2]):
+            j = i + len(TURNED) // 2
+            tiles = [wide[rows, k * BINS : (k + 1) * BINS] for k in (i, j)]
+            out[f * BINS : (f + 1) * BINS] = jnp.concatenate(tiles, axis=0).T
     low = lax.broadcasted_iota(jnp.int32, (BINS, 128), 1) < 64
-    for row in range(0, middle, BINS):
-        a, b = left[row : row + BINS], left[middle + row : middle + row + BINS]
-        first = jnp.where(low, a, pltpu.roll(b, 64, 1))
-        second = jnp.where(low, pltpu.roll(a, 64, 1), b)
-        own[row : row + BINS] = jnp.where(core == 0, first, second)
-        away[row : row + BINS] = jnp.where(core == 0, second, first)
+    a, b = left[:BINS], left[BINS:]
+    first = jnp.where(low, a, pltpu.roll(b, 64, 1))
+    second = jnp.where(low, pltpu.roll(a, 64, 1), b)
+    f = STREAMED[0]
+    own[f * BINS : (f + 1) * BINS] = jnp.where(core == 0, first, second)
+    away[f * BINS : (f + 1) * BINS] = jnp.where(core == 0, second, first)
 
 
 def gain_kernel(target, own, other, spread):
@@ -285,13 +293,13 @@
     depth = LAYERS * HALF
     buffer = [
         pltpu.VMEM((128, depth), BF16),
-        pltpu.VMEM(((FEATS - TURNED) * BINS, depth), BF16),
-        pltpu.VMEM((depth, TURNED * BINS), BF16),
+        pltpu.VMEM((len(STREAMED) * BINS, depth), BF16),
+        pltpu.VMEM((depth, len(TURNED) * BINS), BF16),
     ]
     half = shape(FEATS * BINS // 2, 128)
     own, away = call(
         left_kernel, "left", (half, half), [VMEM], (taken,),
-        scratch=[pltpu.VMEM((FEATS * BINS, 128), F32), pltpu.VMEM((128, TURNED * BINS), F32)] + buffer + buffer, mib=32,
+        scratch=[pltpu.VMEM((len(STREAMED) * BINS, 128), F32), pltpu.VMEM((128, len(TURNED) * BINS), F32)] + buffer + buffer, mib=32,
     )
     other = lax.ppermute(away, "core", [(0, 1), (1, 0)])
     pick_feature, pick_bin, own = lax.optimization_barrier((pick_feature, pick_bin, own))

time: 82.3 us -> 82.1 us (level)
  no operation moved by 1% of the time
where the time goes in v7:
time: 82.1 us; the launch traced here: 80.9 us
  blocking collectives  71.5 us (87%)
  Pallas kernels  7.41 us (9%)
  waiting for transfers between devices  1.05 us (1%)
    all_to_all x1, blocking collectives, per_device(): lax.all_to_all(send, ('xl', 'xh', 'y'), 0, 0, axis_index_groups=neighbour...  25.8 us
    all_to_all x1, blocking collectives, per_device(): came = lax.all_to_all(send, 'z', 0, 0)  24.2 us
    all_to_all x1, blocking collectives, per_device(): gathered = lax.all_to_all(spread, ROW, 0, 0)  16.1 us
    pallas_call x7, Pallas kernels, call(): pl.pallas_call(kernel, out_shape=shapes, in_specs=specs, out_specs=(VMEM,...  7.41 us
    all_gather x1, blocking collectives, per_device(): every = lax.all_gather(joined, CLS)  5.43 us
  transfers between devices with their start and end apart: 1, of which 1 were waited for; matrix products, arithmetic and copies ran while one was open for 0% of the time, Pallas kernels for 0%

profile of v7, /device:TPU:8, one launch (start us, length us, event | category | flops | bytes accessed | tf_op | source)
XLA Modules:
  0.0 80.9 jit_solution(6985766167738858405)
XLA Ops:
  0.6 1.1 %join.1 = (f32[32,256]{1,0:T(8,128)S(1)}, f32[256,128]{1,0:T(8,128)S(1)}, f32[8,128]{1,0:T(8,128)S(1)}, s32[8,128]{1,0:T(8,128)S(1)}) custom-call(f32[16,256]{1,0:T(8,128)} %bitcast.11, s32[16,256]{1,0:T(8,128)} %bitcast.9, s32[1,256]{1,0:T(1,128)} %bitcast.15, s32[256,256]{1,0:T(8,128)} %bins.3, s32[4,16]{1,0:T(4,128)} %bitcast.13, s32[4,16]{1,0:T(4,128)} %bitcast.14), custom_call_target="tpu_custom_call" | custom-call | tf_op jit(solution)/shard_map/join/pallas_call | solution.py:39
  1.7 5.4 %all-gather = f32[128,256]{1,0:T(8,128)S(1)} all-gather(f32[32,256]{1,0:T(8,128)S(1)} %get-tuple-element.16), channel_id=2, replica_groups=mesh['xl'=2,'core'=2,'xh'=2,'z'=8,'y'=4] {'xl','core'}, dimensions={0}, use_global_device_ids=true | all-gather | bytes 163840 | tf_op jit(solution)/shard_map/all_gather | solution.py:288
  7.2 0.1 prepare.1
  7.2 24.2 %all_to_all.15.came = f32[8,104,128]{2,1,0:T(8,128)S(1)} all-to-all(f32[8,104,128]{2,1,0:T(8,128)S(1)} %prepare.1), channel_id=1, replica_groups=mesh['xl'=2,'core'=2,'xh'=2,'z'=8,'y'=4] {'z'}, dimensions={0} | all-to-all | bytes 851968 | tf_op jit(solution)/shard_map/all_to_all | solution.py:290
  31.4 0.1 relay.1
  31.5 25.8 %all_to_all.16.taken = f32[8,328,128]{2,1,0:T(8,128)S(1)} all-to-all(f32[8,328,128]{2,1,0:T(8,128)S(1)} %relay.1), channel_id=1, replica_groups={{0,1,2,3,160,161,162,163},{128,129,130,131,32,33,34,35},{4,5,6,7,164,16..., dimensions={0} | all-to-all | bytes 2686976 | tf_op jit(solution)/shard_map/all_to_all | solution.py:292
  57.3 0.0 copy-start.3
  57.3 0.0 copy-start.4
  57.3 0.0 copy-start
  57.3 0.0 copy-start.1
  57.3 0.0 copy-start.2
  57.3 4.7 %left.1 = (f32[512,128]{1,0:T(8,128)S(1)}, f32[512,128]{1,0:T(8,128)S(1)}) custom-call(f32[8,328,128]{2,1,0:T(8,128)S(1)} %all_to_all.16.taken), custom_call_target="tpu_custom_call" | custom-call | tf_op jit(solution)/shard_map/left/pallas_call | solution.py:39
  62.1 0.1 collective-permute-start
  62.1 0.0 copy-done.3
  62.1 0.1 copy.10
  62.2 0.0 copy-done.4
  62.2 0.1 copy.12
  62.3 0.0 copy-done
  62.3 0.0 copy-done.1
  62.3 0.3 route.1
  62.6 1.1 %collective-permute-done.other = f32[512,128]{1,0:T(8,128)S(1)} collective-permute-done((f32[512,128]{1,0:T(8,128)S(1)}, f32[512,128]{1,0:T(8,128)S(1)}, u32[]{:S(2)}, u32[]{:S(2)}) %collective-permute-start) | collective-permute-done | bytes 262176 | tf_op jit(solution)/shard_map/ppermute | solution.py:304
  63.7 0.3 gain.1
  63.9 16.1 %all_to_all.17.gathered = f32[64,2,128]{2,1,0:T(2,128)S(1)} all-to-all(f32[64,2,128]{2,1,0:T(2,128)S(1)} %gain.1), channel_id=1, replica_groups=mesh['xl'=2,'core'=2,'xh'=2,'z'=8,'y'=4] {'xh','z','y'}, dimensions={0} | all-to-all | bytes 131072 | tf_op jit(solution)/shard_map/all_to_all | solution.py:312
  80.0 0.0 copy-done.2
  80.0 0.9 %finish.1 = (f32[4,16]{1,0:T(4,128)}, f32[16,256]{1,0:T(8,128)}) custom-call(f32[64,2,128]{2,1,0:T(2,128)S(1)} %all_to_all.17.gathered, f32[16,256]{1,0:T(8,128)S(1)} %bitcast.12, s32[16,256]{1,0:T(8,128)S(1)} %route.1), custom_call_target="tpu_custom_call" | custom-call | tf_op jit(solution)/shard_map/finish/pallas_call | solution.py:39
  (1 shorter events, 0.0 us)
Async XLA Ops:
  57.3 4.8 %copy-start.3 = (s32[16,4]{0,1:T(4,128)S(1)}, s32[16,4]{0,1:T(4,128)}, u32[]{:S(2)}) copy-start(s32[16,4]{0,1:T(4,128)} %param.10) | copy-start | bytes 772
  57.3 4.9 %copy-start.4 = (s32[16,4]{0,1:T(4,128)S(1)}, s32[16,4]{0,1:T(4,128)}, u32[]{:S(2)}) copy-start(s32[16,4]{0,1:T(4,128)} %param.11) | copy-start | bytes 772
  57.3 5.0 %copy-start = (s32[256,256]{1,0:T(8,128)S(1)}, s32[256,256]{1,0:T(8,128)}, u32[]{:S(2)}) copy-start(s32[256,256]{1,0:T(8,128)} %bins.3) | copy-start | bytes 786436
  57.3 5.0 %copy-start.1 = (s32[256,16]{0,1:T(8,128)S(1)}, s32[256,16]{0,1:T(8,128)}, u32[]{:S(2)}) copy-start(s32[256,16]{0,1:T(8,128)} %param.8) | copy-start | bytes 49156
  57.3 22.7 %copy-start.2 = (f32[256,16]{0,1:T(8,128)S(1)}, f32[256,16]{0,1:T(8,128)}, u32[]{:S(2)}) copy-start(f32[256,16]{0,1:T(8,128)} %param.6) | copy-start | bytes 49156
  62.1 1.6 %collective-permute-start = (f32[512,128]{1,0:T(8,128)S(1)}, f32[512,128]{1,0:T(8,128)S(1)}, u32[]{:S(2)}, u32[]{:S(2)}) collective-permute-start(f32[512,128]{1,0:T(8,128)S(1)} %get-tuple-element.21), channel_id=1, source_target_pairs={{0,64},{64,0},{1,65},{65,1},{2,66},{66,2},{3,67},{67,3},{4,68},{68... | collective-permute-start | bytes 786440 | tf_op jit(solution)/shard_map/ppermute | solution.py:304

commit v8 on v7

--- a/solution.py
+++ b/solution.py
@@ -166,8 +166,8 @@
                 mask[i * BINS : (i + 1) * BINS, lanes] = masks[f]
 
     def multiply(paired, mask, turned):
+        left[...] += lax.dot_general(mask[...], paired[...], LAST_DIMS, preferred_element_type=F32)
         wide[...] += jnp.dot(paired[...], turned[...], preferred_element_type=F32)
-        left[...] += lax.dot_general(mask[...], paired[...], LAST_DIMS, preferred_element_type=F32)
 
     even, odd = buffers[:3], buffers[3:]
     left[...] = jnp.zeros_like(left)

time: 82.1 us -> 82.1 us (level)
  no operation moved by 1% of the time
where the time goes in v8:
time: 82.1 us; the launch traced here: 80.9 us
  blocking collectives  71.5 us (87%)
  Pallas kernels  7.36 us (9%)
  waiting for transfers between devices  1.05 us (1%)
    all_to_all x1, blocking collectives, per_device(): lax.all_to_all(send, ('xl', 'xh', 'y'), 0, 0, axis_index_groups=neighbour...  25.8 us
    all_to_all x1, blocking collectives, per_device(): came = lax.all_to_all(send, 'z', 0, 0)  24.2 us
    all_to_all x1, blocking collectives, per_device(): gathered = lax.all_to_all(spread, ROW, 0, 0)  16.1 us
    pallas_call x7, Pallas kernels, call(): pl.pallas_call(kernel, out_shape=shapes, in_specs=specs, out_specs=(VMEM,...  7.36 us
    all_gather x1, blocking collectives, per_device(): every = lax.all_gather(joined, CLS)  5.43 us
  transfers between devices with their start and end apart: 1, of which 1 were waited for; matrix products, arithmetic and copies ran while one was open for 0% of the time, Pallas kernels for 0%

profile of v8, /device:TPU:8, one launch (start us, length us, event | category | flops | bytes accessed | tf_op | source)
XLA Modules:
  0.0 80.9 jit_solution(15704406773197797428)
XLA Ops:
  0.6 1.1 %join.1 = (f32[32,256]{1,0:T(8,128)S(1)}, f32[256,128]{1,0:T(8,128)S(1)}, f32[8,128]{1,0:T(8,128)S(1)}, s32[8,128]{1,0:T(8,128)S(1)}) custom-call(f32[16,256]{1,0:T(8,128)} %bitcast.11, s32[16,256]{1,0:T(8,128)} %bitcast.9, s32[1,256]{1,0:T(1,128)} %bitcast.15, s32[256,256]{1,0:T(8,128)} %bins.3, s32[4,16]{1,0:T(4,128)} %bitcast.13, s32[4,16]{1,0:T(4,128)} %bitcast.14), custom_call_target="tpu_custom_call" | custom-call | tf_op jit(solution)/shard_map/join/pallas_call | solution.py:39
  1.7 5.4 %all-gather = f32[128,256]{1,0:T(8,128)S(1)} all-gather(f32[32,256]{1,0:T(8,128)S(1)} %get-tuple-element.16), channel_id=2, replica_groups=mesh['xl'=2,'core'=2,'xh'=2,'z'=8,'y'=4] {'xl','core'}, dimensions={0}, use_global_device_ids=true | all-gather | bytes 163840 | tf_op jit(solution)/shard_map/all_gather | solution.py:288
  7.2 0.1 prepare.1
  7.2 24.2 %all_to_all.15.came = f32[8,104,128]{2,1,0:T(8,128)S(1)} all-to-all(f32[8,104,128]{2,1,0:T(8,128)S(1)} %prepare.1), channel_id=1, replica_groups=mesh['xl'=2,'core'=2,'xh'=2,'z'=8,'y'=4] {'z'}, dimensions={0} | all-to-all | bytes 851968 | tf_op jit(solution)/shard_map/all_to_all | solution.py:290
  31.4 0.1 relay.1
  31.5 25.8 %all_to_all.16.taken = f32[8,328,128]{2,1,0:T(8,128)S(1)} all-to-all(f32[8,328,128]{2,1,0:T(8,128)S(1)} %relay.1), channel_id=1, replica_groups={{0,1,2,3,160,161,162,163},{128,129,130,131,32,33,34,35},{4,5,6,7,164,16..., dimensions={0} | all-to-all | bytes 2686976 | tf_op jit(solution)/shard_map/all_to_all | solution.py:292
  57.3 0.0 copy-start.3
  57.3 0.0 copy-start.4
  57.3 0.0 copy-start
  57.3 0.0 copy-start.1
  57.3 0.0 copy-start.2
  57.3 4.7 %left.1 = (f32[512,128]{1,0:T(8,128)S(1)}, f32[512,128]{1,0:T(8,128)S(1)}) custom-call(f32[8,328,128]{2,1,0:T(8,128)S(1)} %all_to_all.16.taken), custom_call_target="tpu_custom_call" | custom-call | tf_op jit(solution)/shard_map/left/pallas_call | solution.py:39
  62.0 0.1 collective-permute-start
  62.1 0.0 copy-done.3
  62.1 0.1 copy.10
  62.2 0.0 copy-done.4
  62.2 0.1 copy.12
  62.3 0.0 copy-done
  62.3 0.0 copy-done.1
  62.3 0.3 route.1
  62.6 1.1 %collective-permute-done.other = f32[512,128]{1,0:T(8,128)S(1)} collective-permute-done((f32[512,128]{1,0:T(8,128)S(1)}, f32[512,128]{1,0:T(8,128)S(1)}, u32[]{:S(2)}, u32[]{:S(2)}) %collective-permute-start) | collective-permute-done | bytes 262176 | tf_op jit(solution)/shard_map/ppermute | solution.py:304
  63.6 0.3 gain.1
  63.9 16.1 %all_to_all.17.gathered = f32[64,2,128]{2,1,0:T(2,128)S(1)} all-to-all(f32[64,2,128]{2,1,0:T(2,128)S(1)} %gain.1), channel_id=1, replica_groups=mesh['xl'=2,'core'=2,'xh'=2,'z'=8,'y'=4] {'xh','z','y'}, dimensions={0} | all-to-all | bytes 131072 | tf_op jit(solution)/shard_map/all_to_all | solution.py:312
  80.0 0.0 copy-done.2
  80.0 0.9 %finish.1 = (f32[4,16]{1,0:T(4,128)}, f32[16,256]{1,0:T(8,128)}) custom-call(f32[64,2,128]{2,1,0:T(2,128)S(1)} %all_to_all.17.gathered, f32[16,256]{1,0:T(8,128)S(1)} %bitcast.12, s32[16,256]{1,0:T(8,128)S(1)} %route.1), custom_call_target="tpu_custom_call" | custom-call | tf_op jit(solution)/shard_map/finish/pallas_call | solution.py:39
  (1 shorter events, 0.0 us)
Async XLA Ops:
  57.3 4.8 %copy-start.3 = (s32[16,4]{0,1:T(4,128)S(1)}, s32[16,4]{0,1:T(4,128)}, u32[]{:S(2)}) copy-start(s32[16,4]{0,1:T(4,128)} %param.10) | copy-start | bytes 772
  57.3 4.9 %copy-start.4 = (s32[16,4]{0,1:T(4,128)S(1)}, s32[16,4]{0,1:T(4,128)}, u32[]{:S(2)}) copy-start(s32[16,4]{0,1:T(4,128)} %param.11) | copy-start | bytes 772
  57.3 5.0 %copy-start = (s32[256,256]{1,0:T(8,128)S(1)}, s32[256,256]{1,0:T(8,128)}, u32[]{:S(2)}) copy-start(s32[256,256]{1,0:T(8,128)} %bins.3) | copy-start | bytes 786436
  57.3 5.0 %copy-start.1 = (s32[256,16]{0,1:T(8,128)S(1)}, s32[256,16]{0,1:T(8,128)}, u32[]{:S(2)}) copy-start(s32[256,16]{0,1:T(8,128)} %param.8) | copy-start | bytes 49156
  57.3 22.7 %copy-start.2 = (f32[256,16]{0,1:T(8,128)S(1)}, f32[256,16]{0,1:T(8,128)}, u32[]{:S(2)}) copy-start(f32[256,16]{0,1:T(8,128)} %param.6) | copy-start | bytes 49156
  62.0 1.6 %collective-permute-start = (f32[512,128]{1,0:T(8,128)S(1)}, f32[512,128]{1,0:T(8,128)S(1)}, u32[]{:S(2)}, u32[]{:S(2)}) collective-permute-start(f32[512,128]{1,0:T(8,128)S(1)} %get-tuple-element.21), channel_id=1, source_target_pairs={{0,64},{64,0},{1,65},{65,1},{2,66},{66,2},{3,67},{67,3},{4,68},{68... | collective-permute-start | bytes 786440 | tf_op jit(solution)/shard_map/ppermute | solution.py:304
